TPU v7x, 256 devices: a whole 4x4x8 slice. The times are simulated.
256 devices in a mesh: wide: 32 (over y, z_hi, x), narrow: 8 (over z_lo, core).
Axes of the slice: x: 4, y: 4, z: 8 (z_hi: 2, z_lo: 4; z = z_hi * 4 + z_lo), core: 2. Of those that a mesh axis runs over, the one named last changes fastest.
Arguments:
- positions: float32 [32, 8, 3, 2048], P('wide', 'narrow'), may hold values from 0 to 3
- velocities: float32 [32, 8, 3, 2048], P('wide', 'narrow'), may hold values from -3 to 3
- charges: float32 [32, 8, 2048], P('wide', 'narrow'), may hold values from -2.5 to 2.5
- radii: float32 [32, 8, 2048], P('wide', 'narrow'), may hold values from 0.12 to 0.2
- tile_pairs: int32 [32, 8, 2, 256], P('wide', 'narrow'), may hold values from 0 to 79, as said below
- tile_counts: int32 [32, 8], P('wide', 'narrow'), may hold values from 64 to 256, as said below
- destinations: int32 [32, 8, 2048], P('wide', 'narrow'), may hold values from 0 to 8, as said below
Outputs:
- positions_out: float32 [32, 8, 3, 2048], P('wide', 'narrow')
- velocities_out: float32 [32, 8, 3, 2048], P('wide', 'narrow')
- born_radii: float32 [32, 8, 2048], P('wide', 'narrow')
- arrivals: float32 [32, 8, 8, 6, 64], P('wide', 'narrow')
- max_shift: float32 [3], replicated
Inputs may be any that keep to these rules, and one draw needn't show every extreme that they name: `tile_pairs`: in each brick the entries are distinct pairs (local tile, source tile) with local tiles below 16; a source tile below 16 is never below the local tile of its entry. `tile_counts`: 256 is reached in every draw. `destinations`: 0 keeps an atom in its brick; k from 1 to 8 sends it to the brick at the k-th offset of (-1,-1), (-1,0), (-1,1), (0,-1), (0,1), (1,-1), (1,0), (1,1) along (wide, narrow), wrapping around. At most 64 atoms of one brick take one code, and in every draw some brick sends exactly 64 with some code.
All inputs are finite; a program needn't handle non-finite values.
Results may differ from a plain program's by a relative error of at most 0.0003.
Values sent between devices are 32-bit elements; how exact they have to be, the bound alone decides.
No kernel may reach another device: no remote copies, remote signals or barrier semaphores. Data moves between devices by JAX's collectives and lax.ppermute only.
A program may use at most 64 MiB of HBM per device.

v0:
```python
import functools
import jax
import jax.numpy as jnp
from jax import lax
from jax.experimental import pallas as pl
from jax.experimental.pallas import tpu as pltpu
from jax.sharding import PartitionSpec as P

MIGRANTS = 64
STEPS = 3
WIDE = 32
NARROW = 8
AXES = ("wide", "narrow")

scale = 0.4
brick_side = 3.0
step_time = 0.1
skin_depth = 0.2
screen_factor = 0.3
log2e = 1.4426950408889634

ghost_offsets = (
    (0, 0), (0, -1), (0, 1), (-1, -1), (-1, 0), (-1, 1), (1, -1), (1, 0), (1, 1)
)
neighbour_offsets = ((-1, -1), (-1, 0), (-1, 1), (0, -1), (0, 1), (1, -1), (1, 0), (1, 1))
CHUNK = 16
BATCH = 8


def flat_device(x, y, z, core):
    return (y * 8 + (z // 4) * 4 + x) * 8 + (z % 4) * 2 + core


def ring_xz():
    ring = []
    for z in range(8):
        ring += [(x, z) for x in ((1, 2, 3) if z % 2 == 0 else (3, 2, 1))]
    return ring + [(0, z) for z in range(7, -1, -1)]


RING = ring_xz()


def home(w, n):
    return (w % WIDE) * NARROW + n % NARROW


def work(w, n):
    x, z = RING[w % WIDE]
    n = n % NARROW
    return flat_device(x, n if n < 4 else 7 - n, z, 0 if n < 4 else 1)


def send(shard, p=0, s=0, source=work, target=work):
    pairs = [
        (source(w, n), target(w + p, n + s)) for w in range(WIDE) for n in range(NARROW)
    ]
    return lax.ppermute(shard, AXES, pairs)


def device_of(index):
    w, n = divmod(index, NARROW)
    return (w % 4, w // 8, (w // 4) % 2 * 4 + n // 2, n % 2)


def flip_max(value, *flips):
    for flip in flips:
        pairs = []
        for index in range(WIDE * NARROW):
            place = device_of(index)
            pairs.append((index, flat_device(*(a ^ b for a, b in zip(place, flip)))))
        value = jnp.maximum(value, lax.ppermute(value, AXES, pairs))
    return value


def rank_rows(flags):
    rows = flags.shape[0]
    a = lax.broadcasted_iota(jnp.int32, (128, 128), 0)
    b = lax.broadcasted_iota(jnp.int32, (128, 128), 1)
    inside = jnp.dot(
        flags.astype(jnp.bfloat16), (a < b).astype(jnp.bfloat16),
        preferred_element_type=jnp.float32,
    )
    a = lax.broadcasted_iota(jnp.int32, (rows, rows), 0)
    b = lax.broadcasted_iota(jnp.int32, (rows, rows), 1)
    totals = jnp.sum(flags, axis=1, keepdims=True)
    before = jnp.dot(
        (b < a).astype(jnp.bfloat16), jnp.broadcast_to(totals, (rows, 128)).astype(jnp.bfloat16),
        preferred_element_type=jnp.float32,
    )
    return jnp.where(flags > 0, inside + before, -1.0), totals


def compact(candidates, capacity, spare):
    flags = jnp.concatenate([c[0] for c in candidates], axis=0)
    first = jnp.concatenate([c[1] for c in candidates], axis=0)
    second = jnp.concatenate([c[2] for c in candidates], axis=0)
    ranks, totals = rank_rows(flags)
    slots = lax.broadcasted_iota(jnp.int32, (capacity, 128), 0).astype(jnp.float32)
    result = jnp.zeros((16, capacity), jnp.float32)
    for row in range(flags.shape[0]):
        hits = (slots == ranks[row:row + 1]).astype(jnp.bfloat16)
        values = jnp.concatenate(
            [jnp.broadcast_to(first[row:row + 1], (8, 128)),
             jnp.broadcast_to(second[row:row + 1], (8, 128))], axis=0
        ).astype(jnp.bfloat16)
        result = result + lax.dot_general(
            values, hits, (((1,), (1,)), ((), ())), preferred_element_type=jnp.float32
        )
    index = lax.broadcasted_iota(jnp.int32, (8, capacity), 1)
    codes = (result[0:8] * 256.0 + result[8:16]).astype(jnp.int32)
    count = jnp.sum(totals)
    return jnp.where(index < count.astype(jnp.int32), codes, 16 * 256 + spare)[0:1], count


def split_list(listed):
    local, source = listed[0:2], listed[2:4]
    slot = jnp.floor(source * (1.0 / 16.0))
    return local, slot, source - 16.0 * slot


def flag(condition):
    return jnp.where(condition, 1.0, 0.0)


def near_tasks(own_ref, behind_ref, tasks_ref, counts_ref):
    local, slot, tile = split_list(own_ref[...])
    inner = flag(slot == 0.0)
    diagonal = inner * flag(local == tile)
    b_local, b_slot, b_tile = split_list(behind_ref[...])
    plain_tasks, plain = compact(
        [
            (inner - diagonal, local, tile),
            (inner - diagonal, tile, local),
            (flag(slot == 4.0), local, 32.0 + tile),
            (flag(b_slot == 4.0), b_tile, 16.0 + b_local),
        ],
        NEAR_TASKS, 0,
    )
    self_tasks, selves = compact([(diagonal, local, tile)], 128, 0)
    tasks_ref[...] = jnp.concatenate([plain_tasks, self_tasks], axis=1)
    lane = lax.broadcasted_iota(jnp.int32, (8, 128), 1)
    counts_ref[...] = jnp.where(lane == 0, plain, selves).astype(jnp.int32)


def far_tasks(own_ref, behind_ref, tasks_ref, counts_ref):
    local, slot, tile = split_list(own_ref[...])
    ahead = flag(slot >= 1.0) * flag(slot <= 3.0)
    candidates = [(ahead, local, (5.0 + slot) * 16.0 + tile)]
    for brick, want in ((3, 3.0), (4, 2.0), (5, 1.0)):
        b_local, b_slot, b_tile = split_list(behind_ref[brick - 3])
        candidates.append((flag(b_slot == want), b_tile, 16.0 * brick + b_local))
    tasks, count = compact(candidates, FAR_TASKS, 48)
    tasks_ref[...] = tasks
    counts_ref[...] = jnp.broadcast_to(count, (8, 128)).astype(jnp.int32)


NEAR_TASKS = 640
FAR_TASKS = 1152


def make_tasks(kernel, capacity, own_list, behind_list):
    return pl.pallas_call(
        kernel,
        out_shape=(
            jax.ShapeDtypeStruct((1, capacity), jnp.int32),
            jax.ShapeDtypeStruct((8, 128), jnp.int32),
        ),
        compiler_params=pltpu.CompilerParams(vmem_limit_bytes=32 * 1024 * 1024),
    )(own_list, behind_list)


def fill_rows(target, bricks, offsets, component):
    for brick, (value, offset) in enumerate(zip(bricks, offsets)):
        shifted = value * scale
        if component < 2 and offset[component] != 0:
            shifted = (value + brick_side * offset[component]) * scale
        target[pl.ds(brick * 16, 16), :] = shifted


def expand(rows, targets):
    blank = jnp.zeros((128 - rows.shape[0], 128), jnp.float32)
    columns = jnp.transpose(jnp.concatenate([rows, blank], axis=0))
    for component, target in enumerate(targets):
        for tile in range(16):
            lane = component * 16 + tile
            target[tile] = jnp.broadcast_to(columns[:, lane:lane + 1], (128, 128))
        target[16] = jnp.ones((128, 128), jnp.float32)


def collapse(sources):
    lanes = lax.broadcasted_iota(jnp.int32, (128, 128), 1)
    result = jnp.zeros((128, 128), jnp.float32)
    for component, source in enumerate(sources):
        for tile in range(16):
            total = jnp.sum(source[tile], axis=1, keepdims=True)
            result = jnp.where(lanes == component * 16 + tile, total, result)
    return jnp.transpose(result)[0:16 * len(sources)]


def loop_tasks(tasks, count, step):
    def visit(turn, carry):
        for lane in range(BATCH):
            code = tasks[0, turn * BATCH + lane]
            step(lax.shift_right_logical(code, 8), lax.bitwise_and(code, 255))
        return carry

    lax.fori_loop(0, lax.div(count + (BATCH - 1), BATCH), visit, 0)


def loop_single(tasks, begin, count, step):
    def visit(k, carry):
        code = tasks[0, begin + k]
        step(lax.shift_right_logical(code, 8), lax.bitwise_and(code, 255))
        return carry

    lax.fori_loop(0, count, visit, 0)


def not_self(begin):
    a = lax.broadcasted_iota(jnp.int32, (CHUNK, 128), 0) + begin
    b = lax.broadcasted_iota(jnp.int32, (CHUNK, 128), 1)
    return a != b


def screen_kernel(near, counts, tasks, own, radius, ghosts, ghost_radius, prior, out, scratch):
    gx, gy, gz, gr, ex, ey, ez, acc = scratch
    offsets = ghost_offsets[0:3] if near else ghost_offsets[3:9]
    for component, target in enumerate((gx, gy, gz)):
        rows = pl.ds(component * 16, 16)
        bricks = ([own[rows, :]] if near else []) + [ghost[rows, :] for ghost in ghosts]
        fill_rows(target, bricks, offsets, component)
    bricks = ([radius[...]] if near else []) + [ghost[...] for ghost in ghost_radius]
    for brick, value in enumerate(bricks):
        value = value * scale
        gr[pl.ds(brick * 16, 16), :] = value * value
    expand(own[...] * scale, (ex, ey, ez))
    acc[...] = jnp.zeros_like(acc)

    def step(masked, t, g):
        g = g if near else g - 48
        row = pl.ds(g, 1)
        bx, by, bz, br = gx[row, :], gy[row, :], gz[row, :], gr[row, :]
        for begin in range(0, 128, CHUNK):
            part = pl.ds(begin, CHUNK)
            dx = ex[t, part, :] - bx
            dy = ey[t, part, :] - by
            dz = ez[t, part, :] - bz
            u = dx * dx + dy * dy + dz * dz
            h = jnp.maximum(1.0 - u, 0.0)
            value = h * h * br * pl.reciprocal(u + br, approx=True)
            if masked:
                value = jnp.where(not_self(begin), value, 0.0)
            acc[t, part, :] += value

    if near:
        loop_single(tasks, NEAR_TASKS, counts[0, 1], functools.partial(step, True))
        loop_tasks(tasks, counts[0, 0], functools.partial(step, False))
        out[...] = collapse((acc,))
    else:
        loop_tasks(tasks, counts[0, 0], functools.partial(step, False))
        total = screen_factor * (collapse((acc,)) + prior[...])
        out[...] = radius[...] / (1.0 - 0.9 * jnp.tanh(total))


def force_kernel(near, counts, tasks, own, born, charge, ghosts, ghost_born, ghost_charge, extra,
                 outs, scratch):
    gx, gy, gz, gr, gk, gq, ex, ey, ez, er, ek, ax, ay, az = scratch
    offsets = ghost_offsets[0:3] if near else ghost_offsets[3:9]
    for component, target in enumerate((gx, gy, gz)):
        rows = pl.ds(component * 16, 16)
        bricks = ([own[rows, :]] if near else []) + [ghost[rows, :] for ghost in ghosts]
        fill_rows(target, bricks, offsets, component)
    bricks = ([born[...]] if near else []) + [ghost[...] for ghost in ghost_born]
    root = 1.25 * log2e ** 0.5
    for brick, value in enumerate(bricks):
        gr[pl.ds(brick * 16, 16), :] = value * scale
        gk[pl.ds(brick * 16, 16), :] = -root / value
    bricks = ([charge[...]] if near else []) + [ghost[...] for ghost in ghost_charge]
    for brick, value in enumerate(bricks):
        gq[pl.ds(brick * 16, 16), :] = value
    expand(
        jnp.concatenate([own[...] * scale, born[...] * scale, root / born[...]], axis=0),
        (ex, ey, ez, er, ek),
    )
    for acc in (ax, ay, az):
        acc[...] = jnp.zeros_like(acc)

    def step(masked, t, g):
        g = g if near else g - 48
        row = pl.ds(g, 1)
        bx, by, bz = gx[row, :], gy[row, :], gz[row, :]
        br, bk, bq = gr[row, :], gk[row, :], gq[row, :]
        for begin in range(0, 128, CHUNK):
            part = pl.ds(begin, CHUNK)
            dx = ex[t, part, :] - bx
            dy = ey[t, part, :] - by
            dz = ez[t, part, :] - bz
            u = dx * dx + dy * dy + dz * dz
            h = jnp.maximum(1.0 - u, 0.0)
            e = jnp.exp2(u * (ek[t, part, :] * bk))
            inverse = lax.rsqrt(u + er[t, part, :] * br * e)
            w = h * inverse
            c = (bq * w) * (16.0 + (4.0 - e) * (w * inverse))
            if masked:
                c = jnp.where(not_self(begin), c, 0.0)
            ax[t, part, :] += c * dx
            ay[t, part, :] += c * dy
            az[t, part, :] += c * dz

    if near:
        loop_single(tasks, NEAR_TASKS, counts[0, 1], functools.partial(step, True))
        loop_tasks(tasks, counts[0, 0], functools.partial(step, False))
        outs[0][...] = collapse((ax, ay, az))
    else:
        loop_tasks(tasks, counts[0, 0], functools.partial(step, False))
        prior, velocity, anchor = extra
        total = collapse((ax, ay, az)) + prior[...]
        q = jnp.concatenate([charge[...]] * 3, axis=0)
        v = velocity[...] + step_time * (-0.02 * (q * total))
        x = own[...] + step_time * v
        moved = x - anchor[...]
        squared = moved * moved
        squared = squared[0:16] + squared[16:32] + squared[32:48]
        outs[0][...] = x
        outs[1][...] = v
        outs[2][...] = jnp.broadcast_to(jnp.max(jnp.sqrt(squared)), (8, 128))


def vmem(rows=None):
    return pl.BlockSpec(memory_space=pltpu.VMEM)


def smem():
    return pl.BlockSpec(memory_space=pltpu.SMEM)


def params():
    return pltpu.CompilerParams(vmem_limit_bytes=40 * 1024 * 1024)


def tile_scratch(count):
    return [pltpu.VMEM((17, 128, 128), jnp.float32) for _ in range(count)]


def row_scratch(count, bricks):
    return [pltpu.VMEM((bricks * 16, 128), jnp.float32) for _ in range(count)]


def cost(flops):
    return pl.CostEstimate(flops=flops, bytes_accessed=1 << 20, transcendentals=flops // 16)


def screen(near, counts, tasks, own, radius, ghosts, ghost_radius, prior=None):
    many = len(ghosts)
    extra = [] if near else [prior]

    def kernel(*refs):
        counts, tasks, own, radius = refs[0:4]
        ghosts, ghost_radius = refs[4:4 + many], refs[4 + many:4 + 2 * many]
        rest = refs[4 + 2 * many:]
        prior, rest = (None, rest) if near else (rest[0], rest[1:])
        screen_kernel(near, counts, tasks, own, radius, ghosts, ghost_radius, prior, rest[0],
                      rest[1:])

    bricks = 3 if near else 6
    return pl.pallas_call(
        kernel,
        out_shape=jax.ShapeDtypeStruct((16, 128), jnp.float32),
        in_specs=[smem(), smem()] + [vmem()] * (2 + 2 * many + len(extra)),
        out_specs=vmem(),
        scratch_shapes=row_scratch(4, bricks) + tile_scratch(4),
        compiler_params=params(),
        cost_estimate=cost(1 << 26),
    )(counts, tasks, own, radius, *ghosts, *ghost_radius, *extra)


def force(near, counts, tasks, own, born, charge, ghosts, ghost_born, ghost_charge, extra=()):
    many = len(ghosts)

    def kernel(*refs):
        counts, tasks, own, born, charge = refs[0:5]
        rest = refs[5:]
        ghosts, ghost_born, ghost_charge = (
            rest[0:many], rest[many:2 * many], rest[2 * many:3 * many]
        )
        rest = rest[3 * many:]
        extras, rest = rest[0:len(extra)], rest[len(extra):]
        outs = 1 if near else 3
        force_kernel(near, counts, tasks, own, born, charge, ghosts, ghost_born, ghost_charge,
                     extras, rest[0:outs], rest[outs:])

    bricks = 3 if near else 6
    rows = jax.ShapeDtypeStruct((48, 128), jnp.float32)
    out_shape = (rows,) if near else (rows, rows, jax.ShapeDtypeStruct((8, 128), jnp.float32))
    return pl.pallas_call(
        kernel,
        out_shape=out_shape,
        in_specs=[smem(), smem()] + [vmem()] * (3 + 3 * many + len(extra)),
        out_specs=tuple(vmem() for _ in out_shape),
        scratch_shapes=row_scratch(6, bricks) + tile_scratch(8),
        compiler_params=params(),
        cost_estimate=cost(1 << 27),
    )(counts, tasks, own, born, charge, *ghosts, *ghost_born, *ghost_charge, *extra)


def slots_kernel(targets, out):
    codes = targets[...]
    result = jnp.full((16, 128), -1.0, jnp.float32)
    for heading in range(1, 9):
        flags = flag(codes == float(heading))
        ranks, totals = rank_rows(flags)
        result = jnp.where(flags > 0, ranks + float(MIGRANTS * (heading - 1)), result)
    out[...] = result


def migrant_slots(targets):
    return pl.pallas_call(
        slots_kernel, out_shape=jax.ShapeDtypeStruct((16, 128), jnp.float32)
    )(targets)


def pack_kernel(slots, position, velocity, out):
    def parts(value):
        high = value.astype(jnp.bfloat16)
        left = value - high.astype(jnp.float32)
        middle = left.astype(jnp.bfloat16)
        low = (left - middle.astype(jnp.float32)).astype(jnp.bfloat16)
        return high.astype(jnp.float32), middle.astype(jnp.float32), low.astype(jnp.float32)

    split = parts(position[...]), parts(velocity[...])
    wanted = lax.broadcasted_iota(jnp.int32, (8 * MIGRANTS, 128), 0).astype(jnp.float32)
    result = jnp.zeros((32, 8 * MIGRANTS), jnp.float32)
    blank = jnp.zeros((2, 128), jnp.float32)
    for tile in range(16):
        hits = (wanted == slots[tile:tile + 1, :]).astype(jnp.bfloat16)
        rows = []
        for piece in range(3):
            for kind in range(2):
                for component in range(3):
                    row = component * 16 + tile
                    rows.append(split[kind][piece][row:row + 1])
            rows.append(blank)
        rows.append(jnp.zeros((8, 128), jnp.float32))
        state = jnp.concatenate(rows, axis=0).astype(jnp.bfloat16)
        result = result + lax.dot_general(
            state, hits, (((1,), (1,)), ((), ())), preferred_element_type=jnp.float32
        )
    out[...] = (result[0:8] + result[8:16]) + result[16:24]


def pack_migrants(slots, position, velocity):
    table = pl.pallas_call(
        pack_kernel,
        out_shape=jax.ShapeDtypeStruct((8, 8 * MIGRANTS), jnp.float32),
        compiler_params=params(),
    )(slots, position, velocity)
    return jnp.transpose(table[0:6].reshape(6, 8, MIGRANTS), (1, 0, 2))


def across(value):
    return send(value, 0, 1), send(value, 0, -1)


def along(value):
    return send(value, 1, 0), send(value, -1, 0)


def body(positions, velocities, charges, radii, tile_pairs, tile_counts, destinations):
    live = jnp.arange(tile_pairs.shape[3], dtype=jnp.int32) < tile_counts[0, 0]
    listed = jnp.where(live[None], tile_pairs[0, 0], -1).astype(jnp.float32).reshape(4, 128)
    first = jnp.concatenate(
        [
            positions.reshape(48, 128),
            charges.reshape(16, 128),
            radii.reshape(16, 128),
            listed,
            jnp.zeros((4, 128), jnp.float32),
        ]
    )
    later = jnp.concatenate(
        [velocities.reshape(48, 128), destinations.reshape(16, 128).astype(jnp.float32)]
    )
    first = send(first, source=home)
    later = send(later, source=home)
    coords = anchor = first[0:48]
    charge, radius, own_list = first[48:64], first[64:80], first[80:84]
    velocity = later[0:48]
    slots = migrant_slots(later[48:64])

    shifts = []
    for moment in range(STEPS):
        message = first if moment == 0 else coords
        lower, upper = across(message)
        row = jnp.stack([lower, message, upper])
        behind, ahead = along(row)
        if moment == 0:
            near_charge = (lower[48:64], upper[48:64])
            near_radius = (lower[64:80], upper[64:80])
            near_list = make_tasks(near_tasks, NEAR_TASKS + 128, own_list, lower[80:84])
            far_charge = tuple(block[k, 48:64] for block in (behind, ahead) for k in range(3))
            far_radius = tuple(block[k, 64:80] for block in (behind, ahead) for k in range(3))
            far_list = make_tasks(far_tasks, FAR_TASKS, own_list, behind[:, 80:84])
            near_list = (near_list[1], near_list[0])
            far_list = (far_list[1], far_list[0])
        near = (lower[0:48], upper[0:48])
        far = tuple(block[k, 0:48] for block in (behind, ahead) for k in range(3))
        partial = screen(True, *near_list, coords, radius, near, near_radius)
        born = screen(False, *far_list, coords, radius, far, far_radius, partial)
        born_lower, born_upper = across(born)
        row = jnp.stack([born_lower, born, born_upper])
        behind, ahead = along(row)
        far_born = tuple(block[k] for block in (behind, ahead) for k in range(3))
        (partial,) = force(
            True, *near_list, coords, born, charge, near, (born_lower, born_upper), near_charge
        )
        coords, velocity, moved = force(
            False, *far_list, coords, born, charge, far, far_born, far_charge,
            (partial, velocity, anchor),
        )
        shifts.append(moved[0:1])
        if moment == 0:
            slots, velocity = lax.optimization_barrier((slots, velocity))

    outgoing = pack_migrants(slots, coords, velocity)
    shift = jnp.concatenate(shifts, axis=0)
    outgoing, shift = lax.optimization_barrier((outgoing, shift))
    back, forth = send(outgoing[0:3], -1, 0), send(outgoing[5:8], 1, 0)
    shift = flip_max(shift, (0, 0, 0, 1))
    back, forth, shift = lax.optimization_barrier((back, forth, shift))
    down = send(jnp.stack([back[0], outgoing[3], forth[0]]), 0, -1)
    up = send(jnp.stack([back[2], outgoing[4], forth[2]]), 0, 1)
    shift = flip_max(shift, (1, 0, 0, 0))
    down, up, shift = lax.optimization_barrier((down, up, shift))
    arrivals = jnp.stack([down[0], back[1], up[0], down[1], up[1], down[2], forth[1], up[2]])
    rest = jnp.concatenate([coords, velocity, born, arrivals.reshape(24, 128)])
    rest = send(rest, target=home)
    shift = flip_max(shift, (2, 0, 0, 0), (0, 1, 0, 0), (0, 2, 0, 0))
    rest, shift = lax.optimization_barrier((rest, shift))
    shift = flip_max(shift, (0, 0, 1, 0), (0, 0, 2, 0), (0, 0, 4, 0))
    shift = shift[:, 0] / skin_depth
    arrivals = rest[112:136].reshape(8, 6, MIGRANTS)
    return (
        rest[0:48].reshape(1, 1, 3, 2048),
        rest[48:96].reshape(1, 1, 3, 2048),
        rest[96:112].reshape(1, 1, 2048),
        arrivals[None, None],
        shift,
    )


def solution(mesh):
    in_specs = (
        P("wide", "narrow", None, None),
        P("wide", "narrow", None, None),
        P("wide", "narrow", None),
        P("wide", "narrow", None),
        P("wide", "narrow", None, None),
        P("wide", "narrow"),
        P("wide", "narrow", None),
    )
    out_specs = (
        P("wide", "narrow", None, None),
        P("wide", "narrow", None, None),
        P("wide", "narrow", None),
        P("wide", "narrow", None, None, None),
        P(),
    )
    return jax.shard_map(body, mesh=mesh, in_specs=in_specs, out_specs=out_specs, check_vma=False)
```

profile of v0, /device:TPU:16, one launch (start us, length us, event | category | flops | bytes accessed | tf_op | source)
XLA Modules:
  0.0 274.0 jit_solution(8298546185255356648)
XLA Ops:
  1.3 0.7 squeeze.152
  2.1 1.4 concatenate.12
  3.5 9.0 %collective-permute-start = (f32[88,128]{1,0:T(8,128)S(1)}, f32[88,128]{1,0:T(8,128)S(1)}, u32[]{:S(2)}, u32[]{:S(2)}) collective-permute-start(f32[88,128]{1,0:T(8,128)S(1)} %concatenate.12), channel_id=1, source_target_pairs={{0,8},{1,72},{2,136},{3,200},{4,201},{5,137},{6,73},{7,9},{8,16},{... | collective-permute-start | bytes 135176 | tf_op jit(solution)/shard_map/ppermute | solution.py:58
  12.5 3.5 %collective-permute-done = f32[88,128]{1,0:T(8,128)S(1)} collective-permute-done((f32[88,128]{1,0:T(8,128)S(1)}, f32[88,128]{1,0:T(8,128)S(1)}, u32[]{:S(2)}, u32[]{:S(2)}) %collective-permute-start) | collective-permute-done | bytes 45088 | tf_op jit(solution)/shard_map/ppermute | solution.py:58
  15.9 0.5 collective-permute-start.2
  16.5 1.5 collective-permute-start.1
  18.0 2.1 collective-permute-done.2
  20.5 2.7 %collective-permute-start.4 = (f32[3,88,128]{2,1,0:T(8,128)S(1)}, f32[3,88,128]{2,1,0:T(8,128)S(1)}, u32[]{:S(2)}, u32[]{:S(2)}) collective-permute-start(f32[3,88,128]{2,1,0:T(8,128)S(1)} %pad_maximum_fusion), channel_id=1, source_target_pairs={{8,0},{72,64},{136,128},{200,192},{201,193},{137,129},{73,65},{9,1... | collective-permute-start | bytes 405512 | tf_op jit(solution)/shard_map/ppermute | solution.py:58
  23.3 0.9 shard_map.111
  24.2 5.9 %shard_map.112.refs_16_ = f32[16,128]{1,0:T(8,128)S(1)} custom-call(s32[8,128]{1,0:T(8,128)S(1)} %get-tuple-element.32.refs_0_, s32[1,768]{1,0:T(1,128)S(1)} %get-tuple-element.33.refs_1_, f32[48,128]{1,0:T(8,128)S(1)} %slice.350.refs_2_.refs_25_, f32[16,128]{1,0:T(8,128)S(1)} %get-tuple-element.102.refs_3_, f32[48,128]{1,0:T(8,128)S(1)} %slice.365.refs_4_.refs_5_, ...), custom_call_target="tpu_custom_call" | custom-call | flops 67108864 | bytes 1048576 | tf_op jit(solution)/shard_map/pallas_call | solution.py:367
  30.2 1.0 shard_map.110
  31.3 7.8 %shard_map.113.refs_3_ = f32[16,128]{1,0:T(8,128)S(1)} custom-call(s32[8,128]{1,0:T(8,128)S(1)} %get-tuple-element.30.refs_0_, s32[1,1152]{1,0:T(1,128)S(1)} %get-tuple-element.31.refs_1_, f32[48,128]{1,0:T(8,128)S(1)} %slice.350.refs_2_.refs_25_, f32[16,128]{1,0:T(8,128)S(1)} %get-tuple-element.102.refs_3_, ...), custom_call_target="tpu_custom_call" | custom-call | flops 67108864 | bytes 1048576 | tf_op jit(solution)/shard_map/pallas_call | solution.py:367
  39.1 6.1 %collective-permute-start.6 = (f32[16,128]{1,0:T(8,128)S(1)}, f32[16,128]{1,0:T(8,128)S(1)}, u32[]{:S(2)}, u32[]{:S(2)}) collective-permute-start(f32[16,128]{1,0:T(8,128)S(1)} %shard_map.113.refs_3_), channel_id=1, source_target_pairs={{8,9},{72,8},{136,72},{200,136},{201,200},{137,201},{73,137},{9,73... | collective-permute-start | bytes 24584 | tf_op jit(solution)/shard_map/ppermute | solution.py:58
  45.2 8.7 %collective-permute-start.9 = (f32[64,128]{1,0:T(8,128)S(1)}, f32[64,128]{1,0:T(8,128)S(1)}, u32[]{:S(2)}, u32[]{:S(2)}) collective-permute-start(f32[64,128]{1,0:T(8,128)S(1)} %pad_maximum_fusion.4), channel_id=1, source_target_pairs={{0,8},{1,72},{2,136},{3,200},{4,201},{5,137},{6,73},{7,9},{8,16},{... | collective-permute-start | bytes 98312 | tf_op jit(solution)/shard_map/ppermute | solution.py:58
  54.0 1.5 collective-permute-done.9
  55.5 0.5 collective-permute-start.7
  56.0 10.9 %shard_map.114.refs_23_ = f32[48,128]{1,0:T(8,128)S(1)} custom-call(s32[8,128]{1,0:T(8,128)S(1)} %get-tuple-element.32.refs_0_, s32[1,768]{1,0:T(1,128)S(1)} %get-tuple-element.33.refs_1_, f32[48,128]{1,0:T(8,128)S(1)} %slice.350.refs_2_.refs_25_, f32[16,128]{1,0:T(8,128)S(1)} %shard_map.113.refs_3_, f32[16,128]{1,0:T(8,128)S(1)} %get-tuple-element.101.refs_4_, ...), custom_call_target="tpu_custom_call" | custom-call | flops 134217728 | bytes 1048576 | tf_op jit(solution)/shard_map/pallas_call | solution.py:396
  66.9 14.4 %shard_map.115 = (f32[48,128]{1,0:T(8,128)S(1)}, f32[48,128]{1,0:T(8,128)S(1)}, f32[8,128]{1,0:T(8,128)S(1)}) custom-call(s32[8,128]{1,0:T(8,128)S(1)} %get-tuple-element.30.refs_0_, s32[1,1152]{1,0:T(1,128)S(1)} %get-tuple-element.31.refs_1_, f32[48,128]{1,0:T(8,128)S(1)} %slice.350.refs_2_.refs_25_, f32[16,128]{1,0:T(8,128)S(1)} %shard_map.113.refs_3_, ...), custom_call_target="tpu_custom_call" | custom-call | flops 134217728 | bytes 1048576 | tf_op jit(solution)/shard_map/pallas_call | solution.py:396
  81.4 10.7 %collective-permute-start.11 = (f32[48,128]{1,0:T(8,128)S(1)}, f32[48,128]{1,0:T(8,128)S(1)}, u32[]{:S(2)}, u32[]{:S(2)}) collective-permute-start(f32[48,128]{1,0:T(8,128)S(1)} %get-tuple-element.34.refs_2_), channel_id=1, source_target_pairs={{8,9},{72,8},{136,72},{200,136},{201,200},{137,201},{73,137},{9,73... | collective-permute-start | bytes 73736 | tf_op jit(solution)/shard_map/ppermute | solution.py:58
  92.1 1.5 collective-permute-done.11.refs_5_.refs_6_
  93.6 2.3 collective-permute-done.10.refs_4_.refs_5_
  95.9 2.0 collective-permute-start.12
  97.9 5.9 %shard_map.116.refs_16_ = f32[16,128]{1,0:T(8,128)S(1)} custom-call(s32[8,128]{1,0:T(8,128)S(1)} %get-tuple-element.32.refs_0_, s32[1,768]{1,0:T(1,128)S(1)} %get-tuple-element.33.refs_1_, f32[48,128]{1,0:T(8,128)S(1)} %get-tuple-element.34.refs_2_, f32[16,128]{1,0:T(8,128)S(1)} %get-tuple-element.102.refs_3_, ...), custom_call_target="tpu_custom_call" | custom-call | flops 67108864 | bytes 1048576 | tf_op jit(solution)/shard_map/pallas_call | solution.py:367
  103.9 7.8 %shard_map.117.refs_3_ = f32[16,128]{1,0:T(8,128)S(1)} custom-call(s32[8,128]{1,0:T(8,128)S(1)} %get-tuple-element.30.refs_0_, s32[1,1152]{1,0:T(1,128)S(1)} %get-tuple-element.31.refs_1_, f32[48,128]{1,0:T(8,128)S(1)} %get-tuple-element.34.refs_2_, f32[16,128]{1,0:T(8,128)S(1)} %get-tuple-element.102.refs_3_, ...), custom_call_target="tpu_custom_call" | custom-call | flops 67108864 | bytes 1048576 | tf_op jit(solution)/shard_map/pallas_call | solution.py:367
  111.8 4.1 %collective-permute-start.15 = (f32[16,128]{1,0:T(8,128)S(1)}, f32[16,128]{1,0:T(8,128)S(1)}, u32[]{:S(2)}, u32[]{:S(2)}) collective-permute-start(f32[16,128]{1,0:T(8,128)S(1)} %shard_map.117.refs_3_), channel_id=1, source_target_pairs={{8,9},{72,8},{136,72},{200,136},{201,200},{137,201},{73,137},{9,73... | collective-permute-start | bytes 24584 | tf_op jit(solution)/shard_map/ppermute | solution.py:58
  115.9 1.4 collective-permute-done.15.refs_8_
  117.3 2.3 collective-permute-done.14.refs_7_
  119.6 0.6 slice.397.targets
  120.2 1.6 shard_map.119.slots
  121.8 2.0 collective-permute-start.16
  123.8 10.9 %shard_map.118.refs_23_ = f32[48,128]{1,0:T(8,128)S(1)} custom-call(s32[8,128]{1,0:T(8,128)S(1)} %get-tuple-element.32.refs_0_, s32[1,768]{1,0:T(1,128)S(1)} %get-tuple-element.33.refs_1_, f32[48,128]{1,0:T(8,128)S(1)} %get-tuple-element.34.refs_2_, f32[16,128]{1,0:T(8,128)S(1)} %shard_map.117.refs_3_, f32[16,128]{1,0:T(8,128)S(1)} %get-tuple-element.101.refs_4_, ...), custom_call_target="tpu_custom_call" | custom-call | flops 134217728 | bytes 1048576 | tf_op jit(solution)/shard_map/pallas_call | solution.py:396
  134.7 14.4 %shard_map.120 = (f32[48,128]{1,0:T(8,128)S(1)}, f32[48,128]{1,0:T(8,128)S(1)}, f32[8,128]{1,0:T(8,128)S(1)}) custom-call(s32[8,128]{1,0:T(8,128)S(1)} %get-tuple-element.30.refs_0_, s32[1,1152]{1,0:T(1,128)S(1)} %get-tuple-element.31.refs_1_, f32[48,128]{1,0:T(8,128)S(1)} %get-tuple-element.34.refs_2_, f32[16,128]{1,0:T(8,128)S(1)} %shard_map.117.refs_3_, ...), custom_call_target="tpu_custom_call" | custom-call | flops 134217728 | bytes 1048576 | tf_op jit(solution)/shard_map/pallas_call | solution.py:396
  149.2 7.7 %collective-permute-start.19 = (f32[48,128]{1,0:T(8,128)S(1)}, f32[48,128]{1,0:T(8,128)S(1)}, u32[]{:S(2)}, u32[]{:S(2)}) collective-permute-start(f32[48,128]{1,0:T(8,128)S(1)} %get-tuple-element.37.refs_2_), channel_id=1, source_target_pairs={{8,9},{72,8},{136,72},{200,136},{201,200},{137,201},{73,137},{9,73... | collective-permute-start | bytes 73736 | tf_op jit(solution)/shard_map/ppermute | solution.py:58
  156.9 1.5 collective-permute-done.19.refs_5_.refs_6_
  158.4 2.3 collective-permute-done.18.refs_4_.refs_5_
  160.8 2.0 collective-permute-start.20
  162.8 5.9 %shard_map.121.refs_16_ = f32[16,128]{1,0:T(8,128)S(1)} custom-call(s32[8,128]{1,0:T(8,128)S(1)} %get-tuple-element.32.refs_0_, s32[1,768]{1,0:T(1,128)S(1)} %get-tuple-element.33.refs_1_, f32[48,128]{1,0:T(8,128)S(1)} %get-tuple-element.37.refs_2_, f32[16,128]{1,0:T(8,128)S(1)} %get-tuple-element.102.refs_3_, ...), custom_call_target="tpu_custom_call" | custom-call | flops 67108864 | bytes 1048576 | tf_op jit(solution)/shard_map/pallas_call | solution.py:367
  168.8 7.8 %shard_map.122.refs_3_ = f32[16,128]{1,0:T(8,128)S(1)} custom-call(s32[8,128]{1,0:T(8,128)S(1)} %get-tuple-element.30.refs_0_, s32[1,1152]{1,0:T(1,128)S(1)} %get-tuple-element.31.refs_1_, f32[48,128]{1,0:T(8,128)S(1)} %get-tuple-element.37.refs_2_, f32[16,128]{1,0:T(8,128)S(1)} %get-tuple-element.102.refs_3_, ...), custom_call_target="tpu_custom_call" | custom-call | flops 67108864 | bytes 1048576 | tf_op jit(solution)/shard_map/pallas_call | solution.py:367
  176.6 4.1 %collective-permute-start.23 = (f32[16,128]{1,0:T(8,128)S(1)}, f32[16,128]{1,0:T(8,128)S(1)}, u32[]{:S(2)}, u32[]{:S(2)}) collective-permute-start(f32[16,128]{1,0:T(8,128)S(1)} %shard_map.122.refs_3_), channel_id=1, source_target_pairs={{8,9},{72,8},{136,72},{200,136},{201,200},{137,201},{73,137},{9,73... | collective-permute-start | bytes 24584 | tf_op jit(solution)/shard_map/ppermute | solution.py:58
  180.8 1.4 collective-permute-done.23.refs_8_
  182.1 2.3 collective-permute-done.22.refs_7_
  184.4 2.0 collective-permute-start.24
  186.4 10.9 %shard_map.123.refs_23_ = f32[48,128]{1,0:T(8,128)S(1)} custom-call(s32[8,128]{1,0:T(8,128)S(1)} %get-tuple-element.32.refs_0_, s32[1,768]{1,0:T(1,128)S(1)} %get-tuple-element.33.refs_1_, f32[48,128]{1,0:T(8,128)S(1)} %get-tuple-element.37.refs_2_, f32[16,128]{1,0:T(8,128)S(1)} %shard_map.122.refs_3_, f32[16,128]{1,0:T(8,128)S(1)} %get-tuple-element.101.refs_4_, ...), custom_call_target="tpu_custom_call" | custom-call | flops 134217728 | bytes 1048576 | tf_op jit(solution)/shard_map/pallas_call | solution.py:396
  197.4 14.4 %shard_map.124 = (f32[48,128]{1,0:T(8,128)S(1)}, f32[48,128]{1,0:T(8,128)S(1)}, f32[8,128]{1,0:T(8,128)S(1)}) custom-call(s32[8,128]{1,0:T(8,128)S(1)} %get-tuple-element.30.refs_0_, s32[1,1152]{1,0:T(1,128)S(1)} %get-tuple-element.31.refs_1_, f32[48,128]{1,0:T(8,128)S(1)} %get-tuple-element.37.refs_2_, f32[16,128]{1,0:T(8,128)S(1)} %shard_map.122.refs_3_, ...), custom_call_target="tpu_custom_call" | custom-call | flops 134217728 | bytes 1048576 | tf_op jit(solution)/shard_map/pallas_call | solution.py:396
  211.9 0.8 shard_map.125
  213.0 2.0 collective-permute-start.26
  215.1 1.7 collective-permute-done.27
  216.8 7.7 %collective-permute-start.29 = (f32[3,6,64]{2,1,0:T(8,128)S(1)}, f32[3,6,64]{2,1,0:T(8,128)S(1)}, u32[]{:S(2)}, u32[]{:S(2)}) collective-permute-start(f32[3,6,64]{2,1,0:T(8,128)S(1)} %pad_maximum_fusion.8), channel_id=1, source_target_pairs={{8,9},{72,8},{136,72},{200,136},{201,200},{137,201},{73,137},{9,73... | collective-permute-start | bytes 13832 | tf_op jit(solution)/shard_map/ppermute | solution.py:58
  224.7 3.6 %collective-permute-done.31 = f32[3,128]{1,0:T(4,128)S(1)} collective-permute-done((f32[3,128]{1,0:T(4,128)S(1)}, f32[3,128]{1,0:T(4,128)S(1)}, u32[]{:S(2)}, u32[]{:S(2)}) %collective-permute-start.31) | collective-permute-done | bytes 1568 | tf_op jit(solution)/shard_map/ppermute | solution.py:72
  228.4 6.5 %collective-permute-start.32 = (f32[136,128]{1,0:T(8,128)S(1)}, f32[136,128]{1,0:T(8,128)S(1)}, u32[]{:S(2)}, u32[]{:S(2)}) collective-permute-start(f32[136,128]{1,0:T(8,128)S(1)} %pad_maximum_fusion.3), channel_id=1, source_target_pairs={{8,0},{72,1},{136,2},{200,3},{201,4},{137,5},{73,6},{9,7},{16,8},{... | collective-permute-start | bytes 208904 | tf_op jit(solution)/shard_map/ppermute | solution.py:58
  234.9 3.0 %collective-permute-start.33 = (f32[3,128]{1,0:T(4,128)S(1)}, f32[3,128]{1,0:T(4,128)S(1)}, u32[]{:S(2)}, u32[]{:S(2)}) collective-permute-start(f32[3,128]{1,0:T(4,128)S(1)} %max.25), channel_id=1, source_target_pairs={{0,16},{1,17},{2,18},{3,19},{4,20},{5,21},{6,22},{7,23},{8,24},{9,... | collective-permute-start | bytes 4616 | tf_op jit(solution)/shard_map/ppermute | solution.py:72
  237.9 2.1 collective-permute-done.33
  240.0 3.6 %collective-permute-done.34 = f32[3,128]{1,0:T(4,128)S(1)} collective-permute-done((f32[3,128]{1,0:T(4,128)S(1)}, f32[3,128]{1,0:T(4,128)S(1)}, u32[]{:S(2)}, u32[]{:S(2)}) %collective-permute-start.34) | collective-permute-done | bytes 1568 | tf_op jit(solution)/shard_map/ppermute | solution.py:72
  243.6 4.1 %collective-permute-start.35 = (f32[3,128]{1,0:T(4,128)S(1)}, f32[3,128]{1,0:T(4,128)S(1)}, u32[]{:S(2)}, u32[]{:S(2)}) collective-permute-start(f32[3,128]{1,0:T(4,128)S(1)} %max.27), channel_id=1, source_target_pairs={{0,128},{1,129},{2,130},{3,131},{4,132},{5,133},{6,134},{7,135},{8... | collective-permute-start | bytes 4616 | tf_op jit(solution)/shard_map/ppermute | solution.py:72
  247.7 1.6 collective-permute-done.35
  249.3 8.4 %collective-permute-start.36 = (f32[3,128]{1,0:T(4,128)S(1)}, f32[3,128]{1,0:T(4,128)S(1)}, u32[]{:S(2)}, u32[]{:S(2)}) collective-permute-start(f32[3,128]{1,0:T(4,128)S(1)} %max.28), channel_id=1, source_target_pairs={{0,2},{1,3},{2,0},{3,1},{4,6},{5,7},{6,4},{7,5},{8,10},{9,11},{10,... | collective-permute-start | bytes 4616 | tf_op jit(solution)/shard_map/ppermute | solution.py:72
  257.7 1.6 collective-permute-done.36
  259.3 4.6 %collective-permute-start.37 = (f32[3,128]{1,0:T(4,128)S(1)}, f32[3,128]{1,0:T(4,128)S(1)}, u32[]{:S(2)}, u32[]{:S(2)}) collective-permute-start(f32[3,128]{1,0:T(4,128)S(1)} %max.29), channel_id=1, source_target_pairs={{0,4},{1,5},{2,6},{3,7},{4,0},{5,1},{6,2},{7,3},{8,12},{9,13},{10,... | collective-permute-start | bytes 4616 | tf_op jit(solution)/shard_map/ppermute | solution.py:72
  263.9 1.6 collective-permute-done.37
  265.5 0.6 fusion
  266.1 0.6 slice.345
  266.8 0.6 copy.19
  267.4 5.6 %collective-permute-done.38 = f32[3,128]{1,0:T(4,128)S(1)} collective-permute-done((f32[3,128]{1,0:T(4,128)S(1)}, f32[3,128]{1,0:T(4,128)S(1)}, u32[]{:S(2)}, u32[]{:S(2)}) %collective-permute-start.38) | collective-permute-done | bytes 1568 | tf_op jit(solution)/shard_map/ppermute | solution.py:72
  273.0 0.6 multiply_reduce_fusion
  (113 shorter events, 1.6 us)
Async XLA Ops:
  0.6 1.4 copy-start.1
  2.0 10.4 %copy-start.3 = (s32[1,1,2048]{2,1,0:T(1,128)S(1)}, s32[1,1,2048]{2,1,0:T(1,128)}, u32[]{:S(2)}) copy-start(s32[1,1,2048]{2,1,0:T(1,128)} %param.13) | copy-start | bytes 24580
  3.5 12.5 %collective-permute-start = (f32[88,128]{1,0:T(8,128)S(1)}, f32[88,128]{1,0:T(8,128)S(1)}, u32[]{:S(2)}, u32[]{:S(2)}) collective-permute-start(f32[88,128]{1,0:T(8,128)S(1)} %concatenate.12), channel_id=1, source_target_pairs={{0,8},{1,72},{2,136},{3,200},{4,201},{5,137},{6,73},{7,9},{8,16},{... | collective-permute-start | bytes 135176 | tf_op jit(solution)/shard_map/ppermute | solution.py:58
  15.9 4.1 %collective-permute-start.2 = (f32[88,128]{1,0:T(8,128)S(1)}, f32[88,128]{1,0:T(8,128)S(1)}, u32[]{:S(2)}, u32[]{:S(2)}) collective-permute-start(f32[88,128]{1,0:T(8,128)S(1)} %collective-permute-done), channel_id=1, source_target_pairs={{8,9},{72,8},{136,72},{200,136},{201,200},{137,201},{73,137},{9,73... | collective-permute-start | bytes 135176 | tf_op jit(solution)/shard_map/ppermute | solution.py:58
  16.5 4.1 %collective-permute-start.1 = (f32[88,128]{1,0:T(8,128)S(1)}, f32[88,128]{1,0:T(8,128)S(1)}, u32[]{:S(2)}, u32[]{:S(2)}) collective-permute-start(f32[88,128]{1,0:T(8,128)S(1)} %collective-permute-done), channel_id=1, source_target_pairs={{8,72},{72,136},{136,200},{200,201},{201,137},{137,73},{73,9},{9,8... | collective-permute-start | bytes 135176 | tf_op jit(solution)/shard_map/ppermute | solution.py:58
  20.5 10.7 %collective-permute-start.4 = (f32[3,88,128]{2,1,0:T(8,128)S(1)}, f32[3,88,128]{2,1,0:T(8,128)S(1)}, u32[]{:S(2)}, u32[]{:S(2)}) collective-permute-start(f32[3,88,128]{2,1,0:T(8,128)S(1)} %pad_maximum_fusion), channel_id=1, source_target_pairs={{8,0},{72,64},{136,128},{200,192},{201,193},{137,129},{73,65},{9,1... | collective-permute-start | bytes 405512 | tf_op jit(solution)/shard_map/ppermute | solution.py:58
  23.3 6.9 %collective-permute-start.3 = (f32[3,88,128]{2,1,0:T(8,128)S(1)}, f32[3,88,128]{2,1,0:T(8,128)S(1)}, u32[]{:S(2)}, u32[]{:S(2)}) collective-permute-start(f32[3,88,128]{2,1,0:T(8,128)S(1)} %pad_maximum_fusion), channel_id=1, source_target_pairs={{8,16},{72,80},{136,144},{200,208},{201,209},{137,145},{73,81},{9,... | collective-permute-start | bytes 405512 | tf_op jit(solution)/shard_map/ppermute | solution.py:58
  31.3 13.9 %copy-start.2 = (f32[1,1,3,2048]{3,1,2,0:T(1,128)S(1)}, f32[1,1,3,2048]{3,1,2,0:T(1,128)}, u32[]{:S(2)}) copy-start(f32[1,1,3,2048]{3,1,2,0:T(1,128)} %param.8) | copy-start | bytes 73732
  39.1 14.8 %collective-permute-start.6 = (f32[16,128]{1,0:T(8,128)S(1)}, f32[16,128]{1,0:T(8,128)S(1)}, u32[]{:S(2)}, u32[]{:S(2)}) collective-permute-start(f32[16,128]{1,0:T(8,128)S(1)} %shard_map.113.refs_3_), channel_id=1, source_target_pairs={{8,9},{72,8},{136,72},{200,136},{201,200},{137,201},{73,137},{9,73... | collective-permute-start | bytes 24584 | tf_op jit(solution)/shard_map/ppermute | solution.py:58
  45.2 8.7 %collective-permute-start.5 = (f32[16,128]{1,0:T(8,128)S(1)}, f32[16,128]{1,0:T(8,128)S(1)}, u32[]{:S(2)}, u32[]{:S(2)}) collective-permute-start(f32[16,128]{1,0:T(8,128)S(1)} %shard_map.113.refs_3_), channel_id=1, source_target_pairs={{8,72},{72,136},{136,200},{200,201},{201,137},{137,73},{73,9},{9,8... | collective-permute-start | bytes 24584 | tf_op jit(solution)/shard_map/ppermute | solution.py:58
  45.2 10.3 %collective-permute-start.9 = (f32[64,128]{1,0:T(8,128)S(1)}, f32[64,128]{1,0:T(8,128)S(1)}, u32[]{:S(2)}, u32[]{:S(2)}) collective-permute-start(f32[64,128]{1,0:T(8,128)S(1)} %pad_maximum_fusion.4), channel_id=1, source_target_pairs={{0,8},{1,72},{2,136},{3,200},{4,201},{5,137},{6,73},{7,9},{8,16},{... | collective-permute-start | bytes 98312 | tf_op jit(solution)/shard_map/ppermute | solution.py:58
  53.9 13.0 %collective-permute-start.8 = (f32[3,16,128]{2,1,0:T(8,128)S(1)}, f32[3,16,128]{2,1,0:T(8,128)S(1)}, u32[]{:S(2)}, u32[]{:S(2)}) collective-permute-start(f32[3,16,128]{2,1,0:T(8,128)S(1)} %pad_maximum_fusion.5), channel_id=1, source_target_pairs={{8,0},{72,64},{136,128},{200,192},{201,193},{137,129},{73,65},{9,1... | collective-permute-start | bytes 73736 | tf_op jit(solution)/shard_map/ppermute | solution.py:58
  55.5 11.4 %collective-permute-start.7 = (f32[3,16,128]{2,1,0:T(8,128)S(1)}, f32[3,16,128]{2,1,0:T(8,128)S(1)}, u32[]{:S(2)}, u32[]{:S(2)}) collective-permute-start(f32[3,16,128]{2,1,0:T(8,128)S(1)} %pad_maximum_fusion.5), channel_id=1, source_target_pairs={{8,16},{72,80},{136,144},{200,208},{201,209},{137,145},{73,81},{9,... | collective-permute-start | bytes 73736 | tf_op jit(solution)/shard_map/ppermute | solution.py:58
  81.4 12.2 %collective-permute-start.11 = (f32[48,128]{1,0:T(8,128)S(1)}, f32[48,128]{1,0:T(8,128)S(1)}, u32[]{:S(2)}, u32[]{:S(2)}) collective-permute-start(f32[48,128]{1,0:T(8,128)S(1)} %get-tuple-element.34.refs_2_), channel_id=1, source_target_pairs={{8,9},{72,8},{136,72},{200,136},{201,200},{137,201},{73,137},{9,73... | collective-permute-start | bytes 73736 | tf_op jit(solution)/shard_map/ppermute | solution.py:58
  92.1 3.8 %collective-permute-start.10 = (f32[48,128]{1,0:T(8,128)S(1)}, f32[48,128]{1,0:T(8,128)S(1)}, u32[]{:S(2)}, u32[]{:S(2)}) collective-permute-start(f32[48,128]{1,0:T(8,128)S(1)} %get-tuple-element.34.refs_2_), channel_id=1, source_target_pairs={{8,72},{72,136},{136,200},{200,201},{201,137},{137,73},{73,9},{9,8... | collective-permute-start | bytes 73736 | tf_op jit(solution)/shard_map/ppermute | solution.py:58
  95.9 8.0 %collective-permute-start.13 = (f32[3,48,128]{2,1,0:T(8,128)S(1)}, f32[3,48,128]{2,1,0:T(8,128)S(1)}, u32[]{:S(2)}, u32[]{:S(2)}) collective-permute-start(f32[3,48,128]{2,1,0:T(8,128)S(1)} %pad_maximum_fusion.1), channel_id=1, source_target_pairs={{8,0},{72,64},{136,128},{200,192},{201,193},{137,129},{73,65},{9,1... | collective-permute-start | bytes 221192 | tf_op jit(solution)/shard_map/ppermute | solution.py:58
  95.9 8.0 %collective-permute-start.12 = (f32[3,48,128]{2,1,0:T(8,128)S(1)}, f32[3,48,128]{2,1,0:T(8,128)S(1)}, u32[]{:S(2)}, u32[]{:S(2)}) collective-permute-start(f32[3,48,128]{2,1,0:T(8,128)S(1)} %pad_maximum_fusion.1), channel_id=1, source_target_pairs={{8,16},{72,80},{136,144},{200,208},{201,209},{137,145},{73,81},{9,... | collective-permute-start | bytes 221192 | tf_op jit(solution)/shard_map/ppermute | solution.py:58
  111.8 5.5 %collective-permute-start.15 = (f32[16,128]{1,0:T(8,128)S(1)}, f32[16,128]{1,0:T(8,128)S(1)}, u32[]{:S(2)}, u32[]{:S(2)}) collective-permute-start(f32[16,128]{1,0:T(8,128)S(1)} %shard_map.117.refs_3_), channel_id=1, source_target_pairs={{8,9},{72,8},{136,72},{200,136},{201,200},{137,201},{73,137},{9,73... | collective-permute-start | bytes 24584 | tf_op jit(solution)/shard_map/ppermute | solution.py:58
  115.9 3.7 %collective-permute-start.14 = (f32[16,128]{1,0:T(8,128)S(1)}, f32[16,128]{1,0:T(8,128)S(1)}, u32[]{:S(2)}, u32[]{:S(2)}) collective-permute-start(f32[16,128]{1,0:T(8,128)S(1)} %shard_map.117.refs_3_), channel_id=1, source_target_pairs={{8,72},{72,136},{136,200},{200,201},{201,137},{137,73},{73,9},{9,8... | collective-permute-start | bytes 24584 | tf_op jit(solution)/shard_map/ppermute | solution.py:58
  119.6 15.1 %collective-permute-start.17 = (f32[3,16,128]{2,1,0:T(8,128)S(1)}, f32[3,16,128]{2,1,0:T(8,128)S(1)}, u32[]{:S(2)}, u32[]{:S(2)}) collective-permute-start(f32[3,16,128]{2,1,0:T(8,128)S(1)} %pad_maximum_fusion.6), channel_id=1, source_target_pairs={{8,0},{72,64},{136,128},{200,192},{201,193},{137,129},{73,65},{9,1... | collective-permute-start | bytes 73736 | tf_op jit(solution)/shard_map/ppermute | solution.py:58
  121.8 12.9 %collective-permute-start.16 = (f32[3,16,128]{2,1,0:T(8,128)S(1)}, f32[3,16,128]{2,1,0:T(8,128)S(1)}, u32[]{:S(2)}, u32[]{:S(2)}) collective-permute-start(f32[3,16,128]{2,1,0:T(8,128)S(1)} %pad_maximum_fusion.6), channel_id=1, source_target_pairs={{8,16},{72,80},{136,144},{200,208},{201,209},{137,145},{73,81},{9,... | collective-permute-start | bytes 73736 | tf_op jit(solution)/shard_map/ppermute | solution.py:58
  149.2 9.3 %collective-permute-start.19 = (f32[48,128]{1,0:T(8,128)S(1)}, f32[48,128]{1,0:T(8,128)S(1)}, u32[]{:S(2)}, u32[]{:S(2)}) collective-permute-start(f32[48,128]{1,0:T(8,128)S(1)} %get-tuple-element.37.refs_2_), channel_id=1, source_target_pairs={{8,9},{72,8},{136,72},{200,136},{201,200},{137,201},{73,137},{9,73... | collective-permute-start | bytes 73736 | tf_op jit(solution)/shard_map/ppermute | solution.py:58
  156.9 3.8 %collective-permute-start.18 = (f32[48,128]{1,0:T(8,128)S(1)}, f32[48,128]{1,0:T(8,128)S(1)}, u32[]{:S(2)}, u32[]{:S(2)}) collective-permute-start(f32[48,128]{1,0:T(8,128)S(1)} %get-tuple-element.37.refs_2_), channel_id=1, source_target_pairs={{8,72},{72,136},{136,200},{200,201},{201,137},{137,73},{73,9},{9,8... | collective-permute-start | bytes 73736 | tf_op jit(solution)/shard_map/ppermute | solution.py:58
  160.8 8.0 %collective-permute-start.21 = (f32[3,48,128]{2,1,0:T(8,128)S(1)}, f32[3,48,128]{2,1,0:T(8,128)S(1)}, u32[]{:S(2)}, u32[]{:S(2)}) collective-permute-start(f32[3,48,128]{2,1,0:T(8,128)S(1)} %pad_maximum_fusion.2), channel_id=1, source_target_pairs={{8,0},{72,64},{136,128},{200,192},{201,193},{137,129},{73,65},{9,1... | collective-permute-start | bytes 221192 | tf_op jit(solution)/shard_map/ppermute | solution.py:58
  160.8 8.0 %collective-permute-start.20 = (f32[3,48,128]{2,1,0:T(8,128)S(1)}, f32[3,48,128]{2,1,0:T(8,128)S(1)}, u32[]{:S(2)}, u32[]{:S(2)}) collective-permute-start(f32[3,48,128]{2,1,0:T(8,128)S(1)} %pad_maximum_fusion.2), channel_id=1, source_target_pairs={{8,16},{72,80},{136,144},{200,208},{201,209},{137,145},{73,81},{9,... | collective-permute-start | bytes 221192 | tf_op jit(solution)/shard_map/ppermute | solution.py:58
  176.6 5.5 %collective-permute-start.23 = (f32[16,128]{1,0:T(8,128)S(1)}, f32[16,128]{1,0:T(8,128)S(1)}, u32[]{:S(2)}, u32[]{:S(2)}) collective-permute-start(f32[16,128]{1,0:T(8,128)S(1)} %shard_map.122.refs_3_), channel_id=1, source_target_pairs={{8,9},{72,8},{136,72},{200,136},{201,200},{137,201},{73,137},{9,73... | collective-permute-start | bytes 24584 | tf_op jit(solution)/shard_map/ppermute | solution.py:58
  180.8 3.7 %collective-permute-start.22 = (f32[16,128]{1,0:T(8,128)S(1)}, f32[16,128]{1,0:T(8,128)S(1)}, u32[]{:S(2)}, u32[]{:S(2)}) collective-permute-start(f32[16,128]{1,0:T(8,128)S(1)} %shard_map.122.refs_3_), channel_id=1, source_target_pairs={{8,72},{72,136},{136,200},{200,201},{201,137},{137,73},{73,9},{9,8... | collective-permute-start | bytes 24584 | tf_op jit(solution)/shard_map/ppermute | solution.py:58
  184.4 13.0 %collective-permute-start.25 = (f32[3,16,128]{2,1,0:T(8,128)S(1)}, f32[3,16,128]{2,1,0:T(8,128)S(1)}, u32[]{:S(2)}, u32[]{:S(2)}) collective-permute-start(f32[3,16,128]{2,1,0:T(8,128)S(1)} %pad_maximum_fusion.7), channel_id=1, source_target_pairs={{8,0},{72,64},{136,128},{200,192},{201,193},{137,129},{73,65},{9,1... | collective-permute-start | bytes 73736 | tf_op jit(solution)/shard_map/ppermute | solution.py:58
  184.4 13.0 %collective-permute-start.24 = (f32[3,16,128]{2,1,0:T(8,128)S(1)}, f32[3,16,128]{2,1,0:T(8,128)S(1)}, u32[]{:S(2)}, u32[]{:S(2)}) collective-permute-start(f32[3,16,128]{2,1,0:T(8,128)S(1)} %pad_maximum_fusion.7), channel_id=1, source_target_pairs={{8,16},{72,80},{136,144},{200,208},{201,209},{137,145},{73,81},{9,... | collective-permute-start | bytes 73736 | tf_op jit(solution)/shard_map/ppermute | solution.py:58
  197.4 14.5 %copy-start = (f32[16,128]{1,0:T(8,128)S(1)}, f32[16,128]{1,0:T(8,128)}, u32[]{:S(2)}) copy-start(f32[16,128]{1,0:T(8,128)} %shard_map.119.slots) | copy-start | bytes 24580
  212.8 2.2 collective-permute-start.28
  212.9 3.8 %collective-permute-start.27 = (f32[3,6,64]{2,1,0:T(8,128)S(1)}, f32[3,6,64]{2,1,0:T(8,128)S(1)}, u32[]{:S(2)}, u32[]{:S(2)}) collective-permute-start(f32[3,6,64]{2,1,0:T(8,128)S(1)} %get-tuple-element.105), channel_id=1, source_target_pairs={{8,16},{72,80},{136,144},{200,208},{201,209},{137,145},{73,81},{9,... | collective-permute-start | bytes 13832 | tf_op jit(solution)/shard_map/ppermute | solution.py:58
  213.0 3.8 %collective-permute-start.26 = (f32[3,6,64]{2,1,0:T(8,128)S(1)}, f32[3,6,64]{2,1,0:T(8,128)S(1)}, u32[]{:S(2)}, u32[]{:S(2)}) collective-permute-start(f32[3,6,64]{2,1,0:T(8,128)S(1)} %get-tuple-element.106), channel_id=1, source_target_pairs={{8,0},{72,64},{136,128},{200,192},{201,193},{137,129},{73,65},{9,1... | collective-permute-start | bytes 13832 | tf_op jit(solution)/shard_map/ppermute | solution.py:58
  216.8 11.4 %collective-permute-start.29 = (f32[3,6,64]{2,1,0:T(8,128)S(1)}, f32[3,6,64]{2,1,0:T(8,128)S(1)}, u32[]{:S(2)}, u32[]{:S(2)}) collective-permute-start(f32[3,6,64]{2,1,0:T(8,128)S(1)} %pad_maximum_fusion.8), channel_id=1, source_target_pairs={{8,9},{72,8},{136,72},{200,136},{201,200},{137,201},{73,137},{9,73... | collective-permute-start | bytes 13832 | tf_op jit(solution)/shard_map/ppermute | solution.py:58
  224.6 3.7 %collective-permute-start.30 = (f32[3,6,64]{2,1,0:T(8,128)S(1)}, f32[3,6,64]{2,1,0:T(8,128)S(1)}, u32[]{:S(2)}, u32[]{:S(2)}) collective-permute-start(f32[3,6,64]{2,1,0:T(8,128)S(1)} %pad_maximum_fusion.9), channel_id=1, source_target_pairs={{8,72},{72,136},{136,200},{200,201},{201,137},{137,73},{73,9},{9,8... | collective-permute-start | bytes 13832 | tf_op jit(solution)/shard_map/ppermute | solution.py:58
  224.6 3.7 %collective-permute-start.31 = (f32[3,128]{1,0:T(4,128)S(1)}, f32[3,128]{1,0:T(4,128)S(1)}, u32[]{:S(2)}, u32[]{:S(2)}) collective-permute-start(f32[3,128]{1,0:T(4,128)S(1)} %max.24), channel_id=1, source_target_pairs={{0,8},{1,9},{2,10},{3,11},{4,12},{5,13},{6,14},{7,15},{8,0},{9,1},... | collective-permute-start | bytes 4616 | tf_op jit(solution)/shard_map/ppermute | solution.py:72
  228.4 20.9 %collective-permute-start.32 = (f32[136,128]{1,0:T(8,128)S(1)}, f32[136,128]{1,0:T(8,128)S(1)}, u32[]{:S(2)}, u32[]{:S(2)}) collective-permute-start(f32[136,128]{1,0:T(8,128)S(1)} %pad_maximum_fusion.3), channel_id=1, source_target_pairs={{8,0},{72,1},{136,2},{200,3},{201,4},{137,5},{73,6},{9,7},{16,8},{... | collective-permute-start | bytes 208904 | tf_op jit(solution)/shard_map/ppermute | solution.py:58
  234.9 5.1 %collective-permute-start.33 = (f32[3,128]{1,0:T(4,128)S(1)}, f32[3,128]{1,0:T(4,128)S(1)}, u32[]{:S(2)}, u32[]{:S(2)}) collective-permute-start(f32[3,128]{1,0:T(4,128)S(1)} %max.25), channel_id=1, source_target_pairs={{0,16},{1,17},{2,18},{3,19},{4,20},{5,21},{6,22},{7,23},{8,24},{9,... | collective-permute-start | bytes 4616 | tf_op jit(solution)/shard_map/ppermute | solution.py:72
  240.0 3.6 %collective-permute-start.34 = (f32[3,128]{1,0:T(4,128)S(1)}, f32[3,128]{1,0:T(4,128)S(1)}, u32[]{:S(2)}, u32[]{:S(2)}) collective-permute-start(f32[3,128]{1,0:T(4,128)S(1)} %max.26), channel_id=1, source_target_pairs={{0,64},{1,65},{2,66},{3,67},{4,68},{5,69},{6,70},{7,71},{8,72},{9,... | collective-permute-start | bytes 4616 | tf_op jit(solution)/shard_map/ppermute | solution.py:72
  243.6 5.7 %collective-permute-start.35 = (f32[3,128]{1,0:T(4,128)S(1)}, f32[3,128]{1,0:T(4,128)S(1)}, u32[]{:S(2)}, u32[]{:S(2)}) collective-permute-start(f32[3,128]{1,0:T(4,128)S(1)} %max.27), channel_id=1, source_target_pairs={{0,128},{1,129},{2,130},{3,131},{4,132},{5,133},{6,134},{7,135},{8... | collective-permute-start | bytes 4616 | tf_op jit(solution)/shard_map/ppermute | solution.py:72
  249.3 10.0 %collective-permute-start.36 = (f32[3,128]{1,0:T(4,128)S(1)}, f32[3,128]{1,0:T(4,128)S(1)}, u32[]{:S(2)}, u32[]{:S(2)}) collective-permute-start(f32[3,128]{1,0:T(4,128)S(1)} %max.28), channel_id=1, source_target_pairs={{0,2},{1,3},{2,0},{3,1},{4,6},{5,7},{6,4},{7,5},{8,10},{9,11},{10,... | collective-permute-start | bytes 4616 | tf_op jit(solution)/shard_map/ppermute | solution.py:72
  259.3 6.2 %collective-permute-start.37 = (f32[3,128]{1,0:T(4,128)S(1)}, f32[3,128]{1,0:T(4,128)S(1)}, u32[]{:S(2)}, u32[]{:S(2)}) collective-permute-start(f32[3,128]{1,0:T(4,128)S(1)} %max.29), channel_id=1, source_target_pairs={{0,4},{1,5},{2,6},{3,7},{4,0},{5,1},{6,2},{7,3},{8,12},{9,13},{10,... | collective-permute-start | bytes 4616 | tf_op jit(solution)/shard_map/ppermute | solution.py:72
  265.5 7.5 %collective-permute-start.38 = (f32[3,128]{1,0:T(4,128)S(1)}, f32[3,128]{1,0:T(4,128)S(1)}, u32[]{:S(2)}, u32[]{:S(2)}) collective-permute-start(f32[3,128]{1,0:T(4,128)S(1)} %max.30), channel_id=1, source_target_pairs={{0,32},{1,33},{2,34},{3,35},{4,36},{5,37},{6,38},{7,39},{8,40},{9,... | collective-permute-start | bytes 4616 | tf_op jit(solution)/shard_map/ppermute | solution.py:72
where the time goes:
time: 278 us; the launch traced here: 274 us
  Pallas kernels  122 us (44%)
  starting transfers between devices  101 us (36%)
  waiting for transfers between devices  43.8 us (16%)
  local copies, waits for them, and re-layouts  5 us (2%)
    ppermute x31, starting transfers between devices, send(): return lax.ppermute(shard, AXES, pairs)  80.3 us
    pallas_call x6, Pallas kernels, force(): pl.pallas_call(kernel, out_shape=out_shape, in_specs=[smem(), smem()] + [...  76 us
    pallas_call x6, Pallas kernels, screen(): pl.pallas_call(kernel, out_shape=jax.ShapeDtypeStruct((16, 128), jnp.floa...  41.4 us
    ppermute x31, waiting for transfers between devices, send(): return lax.ppermute(shard, AXES, pairs)  24.2 us
    ppermute x8, starting transfers between devices, flip_max(): value = jnp.maximum(value, lax.ppermute(value, AXES, pairs))  20.3 us
    ppermute x8, waiting for transfers between devices, flip_max(): value = jnp.maximum(value, lax.ppermute(value, AXES, pairs))  19.5 us
  transfers between devices with their start and end apart: 39, of which 21 were waited for; matrix products, arithmetic and copies ran while one was open for 1% of the time, Pallas kernels for 20%

commit v1 on v0

--- a/solution.py
+++ b/solution.py
@@ -476,13 +476,12 @@
             radii.reshape(16, 128),
             listed,
             jnp.zeros((4, 128), jnp.float32),
+            velocities.reshape(48, 128),
+            destinations.reshape(16, 128).astype(jnp.float32),
         ]
     )
-    later = jnp.concatenate(
-        [velocities.reshape(48, 128), destinations.reshape(16, 128).astype(jnp.float32)]
-    )
     first = send(first, source=home)
-    later = send(later, source=home)
+    first, later = first[0:88], first[88:152]
     coords = anchor = first[0:48]
     charge, radius, own_list = first[48:64], first[64:80], first[80:84]
     velocity = later[0:48]

time: 278 us -> 281 us (1.011); the launches traced: 274 us -> 280 us
  waiting for transfers between devices: 43.8 us -> 53.9 us
  Pallas kernels: 122 us -> 113 us
  starting transfers between devices: 101 us -> 104 us
    ppermute x31 -> x30, starting transfers between devices: 80.3 us -> 99.7 us  [send(): return lax.ppermute(shard, AXES, pairs)]
    ppermute x8, starting transfers between devices: 20.3 us -> 4.26 us  [flip_max(): value = jnp.maximum(value, lax.ppermute(value, AXES, pairs))]
    ppermute x8, waiting for transfers between devices: 19.5 us -> 26.9 us  [flip_max(): value = jnp.maximum(value, lax.ppermute(value, AXES, pairs))]
    pallas_call x6, Pallas kernels: 76 us -> 70.7 us  [force(): pl.pallas_call(kernel, out_shape=out_shape, in_specs=[smem(), smem()] + [...]
    pallas_call x6, Pallas kernels: 41.4 us -> 38.5 us  [screen(): pl.pallas_call(kernel, out_shape=jax.ShapeDtypeStruct((16, 128), jnp.floa...]
    ppermute x31 -> x30, waiting for transfers between devices: 24.2 us -> 27 us  [send(): return lax.ppermute(shard, AXES, pairs)]
  transfers between devices with their start and end apart: 39 -> 38, of which waited for: 21 -> 21; matrix products, arithmetic and copies ran while one was open for 1% -> 1% of each run, Pallas kernels for 20% -> 19%
where the time goes in v1:
time: 281 us; the launch traced here: 280 us
  Pallas kernels  113 us (40%)
  starting transfers between devices  104 us (37%)
  waiting for transfers between devices  53.9 us (19%)
  local copies, waits for them, and re-layouts  5.01 us (2%)
    ppermute x30, starting transfers between devices, send(): return lax.ppermute(shard, AXES, pairs)  99.7 us
    pallas_call x6, Pallas kernels, force(): pl.pallas_call(kernel, out_shape=out_shape, in_specs=[smem(), smem()] + [...  70.7 us
    pallas_call x6, Pallas kernels, screen(): pl.pallas_call(kernel, out_shape=jax.ShapeDtypeStruct((16, 128), jnp.floa...  38.5 us
    ppermute x30, waiting for transfers between devices, send(): return lax.ppermute(shard, AXES, pairs)  27 us
    ppermute x8, waiting for transfers between devices, flip_max(): value = jnp.maximum(value, lax.ppermute(value, AXES, pairs))  26.9 us
  transfers between devices with their start and end apart: 38, of which 21 were waited for; matrix products, arithmetic and copies ran while one was open for 1% of the time, Pallas kernels for 19%

profile of v1, /device:TPU:16, one launch (start us, length us, event | category | flops | bytes accessed | tf_op | source)
XLA Modules:
  0.0 280.0 jit_solution(5902786451018025378)
XLA Ops:
  1.3 0.7 squeeze.152
  2.0 0.7 convert_element_type.11
  2.8 0.7 copy-done.2
  3.4 0.8 concatenate.9
  4.2 9.0 %collective-permute-start = (f32[152,128]{1,0:T(8,128)S(1)}, f32[152,128]{1,0:T(8,128)S(1)}, u32[]{:S(2)}, u32[]{:S(2)}) collective-permute-start(f32[152,128]{1,0:T(8,128)S(1)} %concatenate.9), channel_id=1, source_target_pairs={{0,8},{1,72},{2,136},{3,200},{4,201},{5,137},{6,73},{7,9},{8,16},{... | collective-permute-start | bytes 233480 | tf_op jit(solution)/shard_map/ppermute | solution.py:58
  13.2 4.9 %collective-permute-done = f32[152,128]{1,0:T(8,128)S(1)} collective-permute-done((f32[152,128]{1,0:T(8,128)S(1)}, f32[152,128]{1,0:T(8,128)S(1)}, u32[]{:S(2)}, u32[]{:S(2)}) %collective-permute-start) | collective-permute-done | bytes 77856 | tf_op jit(solution)/shard_map/ppermute | solution.py:58
  18.1 2.0 collective-permute-start.1
  20.1 0.6 fusion.1
  20.7 1.6 collective-permute-done.2
  22.4 4.5 %collective-permute-start.4 = (f32[3,88,128]{2,1,0:T(8,128)S(1)}, f32[3,88,128]{2,1,0:T(8,128)S(1)}, u32[]{:S(2)}, u32[]{:S(2)}) collective-permute-start(f32[3,88,128]{2,1,0:T(8,128)S(1)} %pad_maximum_fusion), channel_id=1, source_target_pairs={{8,0},{72,64},{136,128},{200,192},{201,193},{137,129},{73,65},{9,1... | collective-permute-start | bytes 405512 | tf_op jit(solution)/shard_map/ppermute | solution.py:58
  26.9 0.9 shard_map.111
  27.9 5.8 %shard_map.112.refs_16_ = f32[16,128]{1,0:T(8,128)S(1)} custom-call(s32[8,128]{1,0:T(8,128)S(1)} %get-tuple-element.32.refs_0_, s32[1,768]{1,0:T(1,128)S(1)} %get-tuple-element.33.refs_1_, f32[48,128]{1,0:T(8,128)S(1)} %get-tuple-element.84.refs_2_.refs_25_, f32[16,128]{1,0:T(8,128)S(1)} %get-tuple-element.87.refs_3_, f32[48,128]{1,0:T(8,128)S(1)} %slice.377.refs_4_.refs_5_, ...), custom_call_target="tpu_custom_call" | custom-call | flops 67108864 | bytes 1048576 | tf_op jit(solution)/shard_map/pallas_call | solution.py:367
  33.7 1.0 shard_map.110
  34.8 7.0 %shard_map.113.refs_3_ = f32[16,128]{1,0:T(8,128)S(1)} custom-call(s32[8,128]{1,0:T(8,128)S(1)} %get-tuple-element.30.refs_0_, s32[1,1152]{1,0:T(1,128)S(1)} %get-tuple-element.31.refs_1_, f32[48,128]{1,0:T(8,128)S(1)} %get-tuple-element.84.refs_2_.refs_25_, f32[16,128]{1,0:T(8,128)S(1)} %get-tuple-element.87.refs_3_, ...), custom_call_target="tpu_custom_call" | custom-call | flops 67108864 | bytes 1048576 | tf_op jit(solution)/shard_map/pallas_call | solution.py:367
  41.8 6.4 %collective-permute-start.6 = (f32[16,128]{1,0:T(8,128)S(1)}, f32[16,128]{1,0:T(8,128)S(1)}, u32[]{:S(2)}, u32[]{:S(2)}) collective-permute-start(f32[16,128]{1,0:T(8,128)S(1)} %shard_map.113.refs_3_), channel_id=1, source_target_pairs={{8,9},{72,8},{136,72},{200,136},{201,200},{137,201},{73,137},{9,73... | collective-permute-start | bytes 24584 | tf_op jit(solution)/shard_map/ppermute | solution.py:58
  48.2 1.4 collective-permute-done.6.refs_8_
  49.6 2.3 collective-permute-done.5.refs_7_
  51.9 2.0 collective-permute-start.7
  53.9 10.7 %shard_map.114.refs_23_ = f32[48,128]{1,0:T(8,128)S(1)} custom-call(s32[8,128]{1,0:T(8,128)S(1)} %get-tuple-element.32.refs_0_, s32[1,768]{1,0:T(1,128)S(1)} %get-tuple-element.33.refs_1_, f32[48,128]{1,0:T(8,128)S(1)} %get-tuple-element.84.refs_2_.refs_25_, f32[16,128]{1,0:T(8,128)S(1)} %shard_map.113.refs_3_, f32[16,128]{1,0:T(8,128)S(1)} %get-tuple-element.85.refs_4_, ...), custom_call_target="tpu_custom_call" | custom-call | flops 134217728 | bytes 1048576 | tf_op jit(solution)/shard_map/pallas_call | solution.py:396
  64.6 12.8 %shard_map.115 = (f32[48,128]{1,0:T(8,128)S(1)}, f32[48,128]{1,0:T(8,128)S(1)}, f32[8,128]{1,0:T(8,128)S(1)}) custom-call(s32[8,128]{1,0:T(8,128)S(1)} %get-tuple-element.30.refs_0_, s32[1,1152]{1,0:T(1,128)S(1)} %get-tuple-element.31.refs_1_, f32[48,128]{1,0:T(8,128)S(1)} %get-tuple-element.84.refs_2_.refs_25_, f32[16,128]{1,0:T(8,128)S(1)} %shard_map.113.refs_3_, ...), custom_call_target="tpu_custom_call" | custom-call | flops 134217728 | bytes 1048576 | tf_op jit(solution)/shard_map/pallas_call | solution.py:396
  77.5 8.5 %collective-permute-start.10 = (f32[48,128]{1,0:T(8,128)S(1)}, f32[48,128]{1,0:T(8,128)S(1)}, u32[]{:S(2)}, u32[]{:S(2)}) collective-permute-start(f32[48,128]{1,0:T(8,128)S(1)} %get-tuple-element.34.refs_2_), channel_id=1, source_target_pairs={{8,9},{72,8},{136,72},{200,136},{201,200},{137,201},{73,137},{9,73... | collective-permute-start | bytes 73736 | tf_op jit(solution)/shard_map/ppermute | solution.py:58
  86.0 1.5 collective-permute-done.10.refs_5_.refs_6_
  87.6 2.3 collective-permute-done.9.refs_4_.refs_5_
  89.9 2.0 collective-permute-start.11
  91.9 5.8 %shard_map.116.refs_16_ = f32[16,128]{1,0:T(8,128)S(1)} custom-call(s32[8,128]{1,0:T(8,128)S(1)} %get-tuple-element.32.refs_0_, s32[1,768]{1,0:T(1,128)S(1)} %get-tuple-element.33.refs_1_, f32[48,128]{1,0:T(8,128)S(1)} %get-tuple-element.34.refs_2_, f32[16,128]{1,0:T(8,128)S(1)} %get-tuple-element.87.refs_3_, ...), custom_call_target="tpu_custom_call" | custom-call | flops 67108864 | bytes 1048576 | tf_op jit(solution)/shard_map/pallas_call | solution.py:367
  97.8 7.0 %shard_map.117.refs_3_ = f32[16,128]{1,0:T(8,128)S(1)} custom-call(s32[8,128]{1,0:T(8,128)S(1)} %get-tuple-element.30.refs_0_, s32[1,1152]{1,0:T(1,128)S(1)} %get-tuple-element.31.refs_1_, f32[48,128]{1,0:T(8,128)S(1)} %get-tuple-element.34.refs_2_, f32[16,128]{1,0:T(8,128)S(1)} %get-tuple-element.87.refs_3_, ...), custom_call_target="tpu_custom_call" | custom-call | flops 67108864 | bytes 1048576 | tf_op jit(solution)/shard_map/pallas_call | solution.py:367
  104.8 4.6 %collective-permute-start.14 = (f32[16,128]{1,0:T(8,128)S(1)}, f32[16,128]{1,0:T(8,128)S(1)}, u32[]{:S(2)}, u32[]{:S(2)}) collective-permute-start(f32[16,128]{1,0:T(8,128)S(1)} %shard_map.117.refs_3_), channel_id=1, source_target_pairs={{8,9},{72,8},{136,72},{200,136},{201,200},{137,201},{73,137},{9,73... | collective-permute-start | bytes 24584 | tf_op jit(solution)/shard_map/ppermute | solution.py:58
  109.4 1.4 collective-permute-done.14.refs_8_
  110.7 2.3 collective-permute-done.13.refs_7_
  113.0 1.6 shard_map.119.slots
  114.6 2.0 collective-permute-start.15
  116.6 10.7 %shard_map.118.refs_23_ = f32[48,128]{1,0:T(8,128)S(1)} custom-call(s32[8,128]{1,0:T(8,128)S(1)} %get-tuple-element.32.refs_0_, s32[1,768]{1,0:T(1,128)S(1)} %get-tuple-element.33.refs_1_, f32[48,128]{1,0:T(8,128)S(1)} %get-tuple-element.34.refs_2_, f32[16,128]{1,0:T(8,128)S(1)} %shard_map.117.refs_3_, f32[16,128]{1,0:T(8,128)S(1)} %get-tuple-element.85.refs_4_, ...), custom_call_target="tpu_custom_call" | custom-call | flops 134217728 | bytes 1048576 | tf_op jit(solution)/shard_map/pallas_call | solution.py:396
  127.4 12.8 %shard_map.120 = (f32[48,128]{1,0:T(8,128)S(1)}, f32[48,128]{1,0:T(8,128)S(1)}, f32[8,128]{1,0:T(8,128)S(1)}) custom-call(s32[8,128]{1,0:T(8,128)S(1)} %get-tuple-element.30.refs_0_, s32[1,1152]{1,0:T(1,128)S(1)} %get-tuple-element.31.refs_1_, f32[48,128]{1,0:T(8,128)S(1)} %get-tuple-element.34.refs_2_, f32[16,128]{1,0:T(8,128)S(1)} %shard_map.117.refs_3_, ...), custom_call_target="tpu_custom_call" | custom-call | flops 134217728 | bytes 1048576 | tf_op jit(solution)/shard_map/pallas_call | solution.py:396
  140.2 8.5 %collective-permute-start.18 = (f32[48,128]{1,0:T(8,128)S(1)}, f32[48,128]{1,0:T(8,128)S(1)}, u32[]{:S(2)}, u32[]{:S(2)}) collective-permute-start(f32[48,128]{1,0:T(8,128)S(1)} %get-tuple-element.37.refs_2_), channel_id=1, source_target_pairs={{8,9},{72,8},{136,72},{200,136},{201,200},{137,201},{73,137},{9,73... | collective-permute-start | bytes 73736 | tf_op jit(solution)/shard_map/ppermute | solution.py:58
  148.8 1.5 collective-permute-done.18.refs_5_.refs_6_
  150.3 2.3 collective-permute-done.17.refs_4_.refs_5_
  152.6 2.0 collective-permute-start.19
  154.6 5.8 %shard_map.121.refs_16_ = f32[16,128]{1,0:T(8,128)S(1)} custom-call(s32[8,128]{1,0:T(8,128)S(1)} %get-tuple-element.32.refs_0_, s32[1,768]{1,0:T(1,128)S(1)} %get-tuple-element.33.refs_1_, f32[48,128]{1,0:T(8,128)S(1)} %get-tuple-element.37.refs_2_, f32[16,128]{1,0:T(8,128)S(1)} %get-tuple-element.87.refs_3_, ...), custom_call_target="tpu_custom_call" | custom-call | flops 67108864 | bytes 1048576 | tf_op jit(solution)/shard_map/pallas_call | solution.py:367
  160.5 7.0 %shard_map.122.refs_3_ = f32[16,128]{1,0:T(8,128)S(1)} custom-call(s32[8,128]{1,0:T(8,128)S(1)} %get-tuple-element.30.refs_0_, s32[1,1152]{1,0:T(1,128)S(1)} %get-tuple-element.31.refs_1_, f32[48,128]{1,0:T(8,128)S(1)} %get-tuple-element.37.refs_2_, f32[16,128]{1,0:T(8,128)S(1)} %get-tuple-element.87.refs_3_, ...), custom_call_target="tpu_custom_call" | custom-call | flops 67108864 | bytes 1048576 | tf_op jit(solution)/shard_map/pallas_call | solution.py:367
  167.5 4.6 %collective-permute-start.22 = (f32[16,128]{1,0:T(8,128)S(1)}, f32[16,128]{1,0:T(8,128)S(1)}, u32[]{:S(2)}, u32[]{:S(2)}) collective-permute-start(f32[16,128]{1,0:T(8,128)S(1)} %shard_map.122.refs_3_), channel_id=1, source_target_pairs={{8,9},{72,8},{136,72},{200,136},{201,200},{137,201},{73,137},{9,73... | collective-permute-start | bytes 24584 | tf_op jit(solution)/shard_map/ppermute | solution.py:58
  172.1 1.4 collective-permute-done.22.refs_8_
  173.5 2.3 collective-permute-done.21.refs_7_
  175.8 2.0 collective-permute-start.23
  177.8 10.8 %shard_map.123.refs_23_ = f32[48,128]{1,0:T(8,128)S(1)} custom-call(s32[8,128]{1,0:T(8,128)S(1)} %get-tuple-element.32.refs_0_, s32[1,768]{1,0:T(1,128)S(1)} %get-tuple-element.33.refs_1_, f32[48,128]{1,0:T(8,128)S(1)} %get-tuple-element.37.refs_2_, f32[16,128]{1,0:T(8,128)S(1)} %shard_map.122.refs_3_, f32[16,128]{1,0:T(8,128)S(1)} %get-tuple-element.85.refs_4_, ...), custom_call_target="tpu_custom_call" | custom-call | flops 134217728 | bytes 1048576 | tf_op jit(solution)/shard_map/pallas_call | solution.py:396
  188.6 12.8 %shard_map.124 = (f32[48,128]{1,0:T(8,128)S(1)}, f32[48,128]{1,0:T(8,128)S(1)}, f32[8,128]{1,0:T(8,128)S(1)}) custom-call(s32[8,128]{1,0:T(8,128)S(1)} %get-tuple-element.30.refs_0_, s32[1,1152]{1,0:T(1,128)S(1)} %get-tuple-element.31.refs_1_, f32[48,128]{1,0:T(8,128)S(1)} %get-tuple-element.37.refs_2_, f32[16,128]{1,0:T(8,128)S(1)} %shard_map.122.refs_3_, ...), custom_call_target="tpu_custom_call" | custom-call | flops 134217728 | bytes 1048576 | tf_op jit(solution)/shard_map/pallas_call | solution.py:396
  201.5 0.8 shard_map.125
  202.8 1.8 collective-permute-start.25
  204.6 1.7 collective-permute-done.26
  206.5 8.4 %collective-permute-start.28 = (f32[3,6,64]{2,1,0:T(8,128)S(1)}, f32[3,6,64]{2,1,0:T(8,128)S(1)}, u32[]{:S(2)}, u32[]{:S(2)}) collective-permute-start(f32[3,6,64]{2,1,0:T(8,128)S(1)} %pad_maximum_fusion.7), channel_id=1, source_target_pairs={{8,9},{72,8},{136,72},{200,136},{201,200},{137,201},{73,137},{9,73... | collective-permute-start | bytes 13832 | tf_op jit(solution)/shard_map/ppermute | solution.py:58
  215.0 3.6 %collective-permute-done.30 = f32[3,128]{1,0:T(4,128)S(1)} collective-permute-done((f32[3,128]{1,0:T(4,128)S(1)}, f32[3,128]{1,0:T(4,128)S(1)}, u32[]{:S(2)}, u32[]{:S(2)}) %collective-permute-start.30) | collective-permute-done | bytes 1568 | tf_op jit(solution)/shard_map/ppermute | solution.py:72
  218.8 30.8 %collective-permute-start.31 = (f32[136,128]{1,0:T(8,128)S(1)}, f32[136,128]{1,0:T(8,128)S(1)}, u32[]{:S(2)}, u32[]{:S(2)}) collective-permute-start(f32[136,128]{1,0:T(8,128)S(1)} %pad_maximum_fusion.3), channel_id=1, source_target_pairs={{8,0},{72,1},{136,2},{200,3},{201,4},{137,5},{73,6},{9,7},{16,8},{... | collective-permute-start | bytes 208904 | tf_op jit(solution)/shard_map/ppermute | solution.py:58
  249.6 5.1 %collective-permute-done.32 = f32[3,128]{1,0:T(4,128)S(1)} collective-permute-done((f32[3,128]{1,0:T(4,128)S(1)}, f32[3,128]{1,0:T(4,128)S(1)}, u32[]{:S(2)}, u32[]{:S(2)}) %collective-permute-start.32) | collective-permute-done | bytes 1568 | tf_op jit(solution)/shard_map/ppermute | solution.py:72
  254.7 3.6 %collective-permute-done.33 = f32[3,128]{1,0:T(4,128)S(1)} collective-permute-done((f32[3,128]{1,0:T(4,128)S(1)}, f32[3,128]{1,0:T(4,128)S(1)}, u32[]{:S(2)}, u32[]{:S(2)}) %collective-permute-start.33) | collective-permute-done | bytes 1568 | tf_op jit(solution)/shard_map/ppermute | solution.py:72
  258.3 2.2 collective-permute-start.34
  260.5 2.8 %collective-permute-done.34 = f32[3,128]{1,0:T(4,128)S(1)} collective-permute-done((f32[3,128]{1,0:T(4,128)S(1)}, f32[3,128]{1,0:T(4,128)S(1)}, u32[]{:S(2)}, u32[]{:S(2)}) %collective-permute-start.34) | collective-permute-done | bytes 1568 | tf_op jit(solution)/shard_map/ppermute | solution.py:72
  263.4 1.0 collective-permute-start.35
  264.4 2.6 collective-permute-done.35
  267.0 0.8 collective-permute-start.36
  267.8 3.7 %collective-permute-done.36 = f32[3,128]{1,0:T(4,128)S(1)} collective-permute-done((f32[3,128]{1,0:T(4,128)S(1)}, f32[3,128]{1,0:T(4,128)S(1)}, u32[]{:S(2)}, u32[]{:S(2)}) %collective-permute-start.36) | collective-permute-done | bytes 1568 | tf_op jit(solution)/shard_map/ppermute | solution.py:72
  271.5 0.6 fusion.2
  272.1 0.6 slice.356
  272.8 0.6 copy.19
  273.4 5.6 %collective-permute-done.37 = f32[3,128]{1,0:T(4,128)S(1)} collective-permute-done((f32[3,128]{1,0:T(4,128)S(1)}, f32[3,128]{1,0:T(4,128)S(1)}, u32[]{:S(2)}, u32[]{:S(2)}) %collective-permute-start.37) | collective-permute-done | bytes 1568 | tf_op jit(solution)/shard_map/ppermute | solution.py:72
  279.0 0.6 multiply_reduce_fusion
  (109 shorter events, 1.3 us)
Async XLA Ops:
  0.6 2.1 copy-start.1
  2.7 0.7 copy-start.2
  2.7 0.7 copy-start.3
  4.2 13.9 %collective-permute-start = (f32[152,128]{1,0:T(8,128)S(1)}, f32[152,128]{1,0:T(8,128)S(1)}, u32[]{:S(2)}, u32[]{:S(2)}) collective-permute-start(f32[152,128]{1,0:T(8,128)S(1)} %concatenate.9), channel_id=1, source_target_pairs={{0,8},{1,72},{2,136},{3,200},{4,201},{5,137},{6,73},{7,9},{8,16},{... | collective-permute-start | bytes 233480 | tf_op jit(solution)/shard_map/ppermute | solution.py:58
  18.1 4.3 %collective-permute-start.2 = (f32[88,128]{1,0:T(8,128)S(1)}, f32[88,128]{1,0:T(8,128)S(1)}, u32[]{:S(2)}, u32[]{:S(2)}) collective-permute-start(f32[88,128]{1,0:T(8,128)S(1)} %get-tuple-element.89), channel_id=1, source_target_pairs={{8,9},{72,8},{136,72},{200,136},{201,200},{137,201},{73,137},{9,73... | collective-permute-start | bytes 135176 | tf_op jit(solution)/shard_map/ppermute | solution.py:58
  18.1 4.3 %collective-permute-start.1 = (f32[88,128]{1,0:T(8,128)S(1)}, f32[88,128]{1,0:T(8,128)S(1)}, u32[]{:S(2)}, u32[]{:S(2)}) collective-permute-start(f32[88,128]{1,0:T(8,128)S(1)} %get-tuple-element.89), channel_id=1, source_target_pairs={{8,72},{72,136},{136,200},{200,201},{201,137},{137,73},{73,9},{9,8... | collective-permute-start | bytes 135176 | tf_op jit(solution)/shard_map/ppermute | solution.py:58
  22.4 12.3 %collective-permute-start.4 = (f32[3,88,128]{2,1,0:T(8,128)S(1)}, f32[3,88,128]{2,1,0:T(8,128)S(1)}, u32[]{:S(2)}, u32[]{:S(2)}) collective-permute-start(f32[3,88,128]{2,1,0:T(8,128)S(1)} %pad_maximum_fusion), channel_id=1, source_target_pairs={{8,0},{72,64},{136,128},{200,192},{201,193},{137,129},{73,65},{9,1... | collective-permute-start | bytes 405512 | tf_op jit(solution)/shard_map/ppermute | solution.py:58
  26.9 6.8 %collective-permute-start.3 = (f32[3,88,128]{2,1,0:T(8,128)S(1)}, f32[3,88,128]{2,1,0:T(8,128)S(1)}, u32[]{:S(2)}, u32[]{:S(2)}) collective-permute-start(f32[3,88,128]{2,1,0:T(8,128)S(1)} %pad_maximum_fusion), channel_id=1, source_target_pairs={{8,16},{72,80},{136,144},{200,208},{201,209},{137,145},{73,81},{9,... | collective-permute-start | bytes 405512 | tf_op jit(solution)/shard_map/ppermute | solution.py:58
  41.8 7.8 %collective-permute-start.6 = (f32[16,128]{1,0:T(8,128)S(1)}, f32[16,128]{1,0:T(8,128)S(1)}, u32[]{:S(2)}, u32[]{:S(2)}) collective-permute-start(f32[16,128]{1,0:T(8,128)S(1)} %shard_map.113.refs_3_), channel_id=1, source_target_pairs={{8,9},{72,8},{136,72},{200,136},{201,200},{137,201},{73,137},{9,73... | collective-permute-start | bytes 24584 | tf_op jit(solution)/shard_map/ppermute | solution.py:58
  48.2 3.7 %collective-permute-start.5 = (f32[16,128]{1,0:T(8,128)S(1)}, f32[16,128]{1,0:T(8,128)S(1)}, u32[]{:S(2)}, u32[]{:S(2)}) collective-permute-start(f32[16,128]{1,0:T(8,128)S(1)} %shard_map.113.refs_3_), channel_id=1, source_target_pairs={{8,72},{72,136},{136,200},{200,201},{201,137},{137,73},{73,9},{9,8... | collective-permute-start | bytes 24584 | tf_op jit(solution)/shard_map/ppermute | solution.py:58
  51.9 12.7 %collective-permute-start.8 = (f32[3,16,128]{2,1,0:T(8,128)S(1)}, f32[3,16,128]{2,1,0:T(8,128)S(1)}, u32[]{:S(2)}, u32[]{:S(2)}) collective-permute-start(f32[3,16,128]{2,1,0:T(8,128)S(1)} %pad_maximum_fusion.4), channel_id=1, source_target_pairs={{8,0},{72,64},{136,128},{200,192},{201,193},{137,129},{73,65},{9,1... | collective-permute-start | bytes 73736 | tf_op jit(solution)/shard_map/ppermute | solution.py:58
  51.9 12.7 %collective-permute-start.7 = (f32[3,16,128]{2,1,0:T(8,128)S(1)}, f32[3,16,128]{2,1,0:T(8,128)S(1)}, u32[]{:S(2)}, u32[]{:S(2)}) collective-permute-start(f32[3,16,128]{2,1,0:T(8,128)S(1)} %pad_maximum_fusion.4), channel_id=1, source_target_pairs={{8,16},{72,80},{136,144},{200,208},{201,209},{137,145},{73,81},{9,... | collective-permute-start | bytes 73736 | tf_op jit(solution)/shard_map/ppermute | solution.py:58
  77.5 10.1 %collective-permute-start.10 = (f32[48,128]{1,0:T(8,128)S(1)}, f32[48,128]{1,0:T(8,128)S(1)}, u32[]{:S(2)}, u32[]{:S(2)}) collective-permute-start(f32[48,128]{1,0:T(8,128)S(1)} %get-tuple-element.34.refs_2_), channel_id=1, source_target_pairs={{8,9},{72,8},{136,72},{200,136},{201,200},{137,201},{73,137},{9,73... | collective-permute-start | bytes 73736 | tf_op jit(solution)/shard_map/ppermute | solution.py:58
  86.0 3.8 %collective-permute-start.9 = (f32[48,128]{1,0:T(8,128)S(1)}, f32[48,128]{1,0:T(8,128)S(1)}, u32[]{:S(2)}, u32[]{:S(2)}) collective-permute-start(f32[48,128]{1,0:T(8,128)S(1)} %get-tuple-element.34.refs_2_), channel_id=1, source_target_pairs={{8,72},{72,136},{136,200},{200,201},{201,137},{137,73},{73,9},{9,8... | collective-permute-start | bytes 73736 | tf_op jit(solution)/shard_map/ppermute | solution.py:58
  89.9 7.9 %collective-permute-start.12 = (f32[3,48,128]{2,1,0:T(8,128)S(1)}, f32[3,48,128]{2,1,0:T(8,128)S(1)}, u32[]{:S(2)}, u32[]{:S(2)}) collective-permute-start(f32[3,48,128]{2,1,0:T(8,128)S(1)} %pad_maximum_fusion.1), channel_id=1, source_target_pairs={{8,0},{72,64},{136,128},{200,192},{201,193},{137,129},{73,65},{9,1... | collective-permute-start | bytes 221192 | tf_op jit(solution)/shard_map/ppermute | solution.py:58
  89.9 7.9 %collective-permute-start.11 = (f32[3,48,128]{2,1,0:T(8,128)S(1)}, f32[3,48,128]{2,1,0:T(8,128)S(1)}, u32[]{:S(2)}, u32[]{:S(2)}) collective-permute-start(f32[3,48,128]{2,1,0:T(8,128)S(1)} %pad_maximum_fusion.1), channel_id=1, source_target_pairs={{8,16},{72,80},{136,144},{200,208},{201,209},{137,145},{73,81},{9,... | collective-permute-start | bytes 221192 | tf_op jit(solution)/shard_map/ppermute | solution.py:58
  104.8 5.9 %collective-permute-start.14 = (f32[16,128]{1,0:T(8,128)S(1)}, f32[16,128]{1,0:T(8,128)S(1)}, u32[]{:S(2)}, u32[]{:S(2)}) collective-permute-start(f32[16,128]{1,0:T(8,128)S(1)} %shard_map.117.refs_3_), channel_id=1, source_target_pairs={{8,9},{72,8},{136,72},{200,136},{201,200},{137,201},{73,137},{9,73... | collective-permute-start | bytes 24584 | tf_op jit(solution)/shard_map/ppermute | solution.py:58
  109.4 3.7 %collective-permute-start.13 = (f32[16,128]{1,0:T(8,128)S(1)}, f32[16,128]{1,0:T(8,128)S(1)}, u32[]{:S(2)}, u32[]{:S(2)}) collective-permute-start(f32[16,128]{1,0:T(8,128)S(1)} %shard_map.117.refs_3_), channel_id=1, source_target_pairs={{8,72},{72,136},{136,200},{200,201},{201,137},{137,73},{73,9},{9,8... | collective-permute-start | bytes 24584 | tf_op jit(solution)/shard_map/ppermute | solution.py:58
  113.0 14.3 %collective-permute-start.16 = (f32[3,16,128]{2,1,0:T(8,128)S(1)}, f32[3,16,128]{2,1,0:T(8,128)S(1)}, u32[]{:S(2)}, u32[]{:S(2)}) collective-permute-start(f32[3,16,128]{2,1,0:T(8,128)S(1)} %pad_maximum_fusion.5), channel_id=1, source_target_pairs={{8,0},{72,64},{136,128},{200,192},{201,193},{137,129},{73,65},{9,1... | collective-permute-start | bytes 73736 | tf_op jit(solution)/shard_map/ppermute | solution.py:58
  114.6 12.8 %collective-permute-start.15 = (f32[3,16,128]{2,1,0:T(8,128)S(1)}, f32[3,16,128]{2,1,0:T(8,128)S(1)}, u32[]{:S(2)}, u32[]{:S(2)}) collective-permute-start(f32[3,16,128]{2,1,0:T(8,128)S(1)} %pad_maximum_fusion.5), channel_id=1, source_target_pairs={{8,16},{72,80},{136,144},{200,208},{201,209},{137,145},{73,81},{9,... | collective-permute-start | bytes 73736 | tf_op jit(solution)/shard_map/ppermute | solution.py:58
  140.2 10.1 %collective-permute-start.18 = (f32[48,128]{1,0:T(8,128)S(1)}, f32[48,128]{1,0:T(8,128)S(1)}, u32[]{:S(2)}, u32[]{:S(2)}) collective-permute-start(f32[48,128]{1,0:T(8,128)S(1)} %get-tuple-element.37.refs_2_), channel_id=1, source_target_pairs={{8,9},{72,8},{136,72},{200,136},{201,200},{137,201},{73,137},{9,73... | collective-permute-start | bytes 73736 | tf_op jit(solution)/shard_map/ppermute | solution.py:58
  148.8 3.8 %collective-permute-start.17 = (f32[48,128]{1,0:T(8,128)S(1)}, f32[48,128]{1,0:T(8,128)S(1)}, u32[]{:S(2)}, u32[]{:S(2)}) collective-permute-start(f32[48,128]{1,0:T(8,128)S(1)} %get-tuple-element.37.refs_2_), channel_id=1, source_target_pairs={{8,72},{72,136},{136,200},{200,201},{201,137},{137,73},{73,9},{9,8... | collective-permute-start | bytes 73736 | tf_op jit(solution)/shard_map/ppermute | solution.py:58
  152.6 7.9 %collective-permute-start.20 = (f32[3,48,128]{2,1,0:T(8,128)S(1)}, f32[3,48,128]{2,1,0:T(8,128)S(1)}, u32[]{:S(2)}, u32[]{:S(2)}) collective-permute-start(f32[3,48,128]{2,1,0:T(8,128)S(1)} %pad_maximum_fusion.2), channel_id=1, source_target_pairs={{8,0},{72,64},{136,128},{200,192},{201,193},{137,129},{73,65},{9,1... | collective-permute-start | bytes 221192 | tf_op jit(solution)/shard_map/ppermute | solution.py:58
  152.6 7.9 %collective-permute-start.19 = (f32[3,48,128]{2,1,0:T(8,128)S(1)}, f32[3,48,128]{2,1,0:T(8,128)S(1)}, u32[]{:S(2)}, u32[]{:S(2)}) collective-permute-start(f32[3,48,128]{2,1,0:T(8,128)S(1)} %pad_maximum_fusion.2), channel_id=1, source_target_pairs={{8,16},{72,80},{136,144},{200,208},{201,209},{137,145},{73,81},{9,... | collective-permute-start | bytes 221192 | tf_op jit(solution)/shard_map/ppermute | solution.py:58
  167.5 5.9 %collective-permute-start.22 = (f32[16,128]{1,0:T(8,128)S(1)}, f32[16,128]{1,0:T(8,128)S(1)}, u32[]{:S(2)}, u32[]{:S(2)}) collective-permute-start(f32[16,128]{1,0:T(8,128)S(1)} %shard_map.122.refs_3_), channel_id=1, source_target_pairs={{8,9},{72,8},{136,72},{200,136},{201,200},{137,201},{73,137},{9,73... | collective-permute-start | bytes 24584 | tf_op jit(solution)/shard_map/ppermute | solution.py:58
  172.1 3.7 %collective-permute-start.21 = (f32[16,128]{1,0:T(8,128)S(1)}, f32[16,128]{1,0:T(8,128)S(1)}, u32[]{:S(2)}, u32[]{:S(2)}) collective-permute-start(f32[16,128]{1,0:T(8,128)S(1)} %shard_map.122.refs_3_), channel_id=1, source_target_pairs={{8,72},{72,136},{136,200},{200,201},{201,137},{137,73},{73,9},{9,8... | collective-permute-start | bytes 24584 | tf_op jit(solution)/shard_map/ppermute | solution.py:58
  175.7 12.8 %collective-permute-start.24 = (f32[3,16,128]{2,1,0:T(8,128)S(1)}, f32[3,16,128]{2,1,0:T(8,128)S(1)}, u32[]{:S(2)}, u32[]{:S(2)}) collective-permute-start(f32[3,16,128]{2,1,0:T(8,128)S(1)} %pad_maximum_fusion.6), channel_id=1, source_target_pairs={{8,0},{72,64},{136,128},{200,192},{201,193},{137,129},{73,65},{9,1... | collective-permute-start | bytes 73736 | tf_op jit(solution)/shard_map/ppermute | solution.py:58
  175.8 12.8 %collective-permute-start.23 = (f32[3,16,128]{2,1,0:T(8,128)S(1)}, f32[3,16,128]{2,1,0:T(8,128)S(1)}, u32[]{:S(2)}, u32[]{:S(2)}) collective-permute-start(f32[3,16,128]{2,1,0:T(8,128)S(1)} %pad_maximum_fusion.6), channel_id=1, source_target_pairs={{8,16},{72,80},{136,144},{200,208},{201,209},{137,145},{73,81},{9,... | collective-permute-start | bytes 73736 | tf_op jit(solution)/shard_map/ppermute | solution.py:58
  188.6 12.9 %copy-start = (f32[16,128]{1,0:T(8,128)S(1)}, f32[16,128]{1,0:T(8,128)}, u32[]{:S(2)}) copy-start(f32[16,128]{1,0:T(8,128)} %shard_map.119.slots) | copy-start | bytes 24580
  202.4 2.2 collective-permute-start.27
  202.5 3.8 %collective-permute-start.26 = (f32[3,6,64]{2,1,0:T(8,128)S(1)}, f32[3,6,64]{2,1,0:T(8,128)S(1)}, u32[]{:S(2)}, u32[]{:S(2)}) collective-permute-start(f32[3,6,64]{2,1,0:T(8,128)S(1)} %get-tuple-element.110), channel_id=1, source_target_pairs={{8,16},{72,80},{136,144},{200,208},{201,209},{137,145},{73,81},{9,... | collective-permute-start | bytes 13832 | tf_op jit(solution)/shard_map/ppermute | solution.py:58
  202.8 3.7 %collective-permute-start.25 = (f32[3,6,64]{2,1,0:T(8,128)S(1)}, f32[3,6,64]{2,1,0:T(8,128)S(1)}, u32[]{:S(2)}, u32[]{:S(2)}) collective-permute-start(f32[3,6,64]{2,1,0:T(8,128)S(1)} %get-tuple-element.111), channel_id=1, source_target_pairs={{8,0},{72,64},{136,128},{200,192},{201,193},{137,129},{73,65},{9,1... | collective-permute-start | bytes 13832 | tf_op jit(solution)/shard_map/ppermute | solution.py:58
  206.5 12.1 %collective-permute-start.28 = (f32[3,6,64]{2,1,0:T(8,128)S(1)}, f32[3,6,64]{2,1,0:T(8,128)S(1)}, u32[]{:S(2)}, u32[]{:S(2)}) collective-permute-start(f32[3,6,64]{2,1,0:T(8,128)S(1)} %pad_maximum_fusion.7), channel_id=1, source_target_pairs={{8,9},{72,8},{136,72},{200,136},{201,200},{137,201},{73,137},{9,73... | collective-permute-start | bytes 13832 | tf_op jit(solution)/shard_map/ppermute | solution.py:58
  214.9 3.7 %collective-permute-start.29 = (f32[3,6,64]{2,1,0:T(8,128)S(1)}, f32[3,6,64]{2,1,0:T(8,128)S(1)}, u32[]{:S(2)}, u32[]{:S(2)}) collective-permute-start(f32[3,6,64]{2,1,0:T(8,128)S(1)} %pad_maximum_fusion.8), channel_id=1, source_target_pairs={{8,72},{72,136},{136,200},{200,201},{201,137},{137,73},{73,9},{9,8... | collective-permute-start | bytes 13832 | tf_op jit(solution)/shard_map/ppermute | solution.py:58
  214.9 3.7 %collective-permute-start.30 = (f32[3,128]{1,0:T(4,128)S(1)}, f32[3,128]{1,0:T(4,128)S(1)}, u32[]{:S(2)}, u32[]{:S(2)}) collective-permute-start(f32[3,128]{1,0:T(4,128)S(1)} %max.24), channel_id=1, source_target_pairs={{0,8},{1,9},{2,10},{3,11},{4,12},{5,13},{6,14},{7,15},{8,0},{9,1},... | collective-permute-start | bytes 4616 | tf_op jit(solution)/shard_map/ppermute | solution.py:72
  218.8 44.6 %collective-permute-start.31 = (f32[136,128]{1,0:T(8,128)S(1)}, f32[136,128]{1,0:T(8,128)S(1)}, u32[]{:S(2)}, u32[]{:S(2)}) collective-permute-start(f32[136,128]{1,0:T(8,128)S(1)} %pad_maximum_fusion.3), channel_id=1, source_target_pairs={{8,0},{72,1},{136,2},{200,3},{201,4},{137,5},{73,6},{9,7},{16,8},{... | collective-permute-start | bytes 208904 | tf_op jit(solution)/shard_map/ppermute | solution.py:58
  249.6 5.1 %collective-permute-start.32 = (f32[3,128]{1,0:T(4,128)S(1)}, f32[3,128]{1,0:T(4,128)S(1)}, u32[]{:S(2)}, u32[]{:S(2)}) collective-permute-start(f32[3,128]{1,0:T(4,128)S(1)} %max.25), channel_id=1, source_target_pairs={{0,16},{1,17},{2,18},{3,19},{4,20},{5,21},{6,22},{7,23},{8,24},{9,... | collective-permute-start | bytes 4616 | tf_op jit(solution)/shard_map/ppermute | solution.py:72
  254.7 3.6 %collective-permute-start.33 = (f32[3,128]{1,0:T(4,128)S(1)}, f32[3,128]{1,0:T(4,128)S(1)}, u32[]{:S(2)}, u32[]{:S(2)}) collective-permute-start(f32[3,128]{1,0:T(4,128)S(1)} %max.26), channel_id=1, source_target_pairs={{0,64},{1,65},{2,66},{3,67},{4,68},{5,69},{6,70},{7,71},{8,72},{9,... | collective-permute-start | bytes 4616 | tf_op jit(solution)/shard_map/ppermute | solution.py:72
  258.3 5.1 %collective-permute-start.34 = (f32[3,128]{1,0:T(4,128)S(1)}, f32[3,128]{1,0:T(4,128)S(1)}, u32[]{:S(2)}, u32[]{:S(2)}) collective-permute-start(f32[3,128]{1,0:T(4,128)S(1)} %max.27), channel_id=1, source_target_pairs={{0,128},{1,129},{2,130},{3,131},{4,132},{5,133},{6,134},{7,135},{8... | collective-permute-start | bytes 4616 | tf_op jit(solution)/shard_map/ppermute | solution.py:72
  263.4 3.6 %collective-permute-start.35 = (f32[3,128]{1,0:T(4,128)S(1)}, f32[3,128]{1,0:T(4,128)S(1)}, u32[]{:S(2)}, u32[]{:S(2)}) collective-permute-start(f32[3,128]{1,0:T(4,128)S(1)} %max.28), channel_id=1, source_target_pairs={{0,2},{1,3},{2,0},{3,1},{4,6},{5,7},{6,4},{7,5},{8,10},{9,11},{10,... | collective-permute-start | bytes 4616 | tf_op jit(solution)/shard_map/ppermute | solution.py:72
  267.0 4.5 %collective-permute-start.36 = (f32[3,128]{1,0:T(4,128)S(1)}, f32[3,128]{1,0:T(4,128)S(1)}, u32[]{:S(2)}, u32[]{:S(2)}) collective-permute-start(f32[3,128]{1,0:T(4,128)S(1)} %max.29), channel_id=1, source_target_pairs={{0,4},{1,5},{2,6},{3,7},{4,0},{5,1},{6,2},{7,3},{8,12},{9,13},{10,... | collective-permute-start | bytes 4616 | tf_op jit(solution)/shard_map/ppermute | solution.py:72
  271.5 7.5 %collective-permute-start.37 = (f32[3,128]{1,0:T(4,128)S(1)}, f32[3,128]{1,0:T(4,128)S(1)}, u32[]{:S(2)}, u32[]{:S(2)}) collective-permute-start(f32[3,128]{1,0:T(4,128)S(1)} %max.30), channel_id=1, source_target_pairs={{0,32},{1,33},{2,34},{3,35},{4,36},{5,37},{6,38},{7,39},{8,40},{9,... | collective-permute-start | bytes 4616 | tf_op jit(solution)/shard_map/ppermute | solution.py:72
